TPU v7x, 32 devices: a whole 2x2x4 slice. The times are simulated.
32 devices in a mesh: axial: 4 (over y, x), cross: 8 (over z, core).
Axes of the slice: x: 2, y: 2, z: 4, core: 2. Of those that a mesh axis runs over, the one named last changes fastest.
Arguments:
- force: float32 [4, 8, 8, 3, 128], P('axial', 'cross'), may hold values from -6 to 6
- self_drag: float32 [4, 8, 8, 128], P('axial', 'cross'), may hold values from 0.5 to 4
- tiles: bfloat16 [4, 8, 8, 8, 128, 128], P('axial', 'cross'), may hold values from -0.1875 to 0.1875
- tile_ids: int32 [4, 8, 8, 8], P('axial', 'cross'), may hold values from 8 to 63, as said below
- mig_rows: int32 [4, 8, 2, 64], P('axial', 'cross'), may hold values from 0 to 1023, as said below
- mig_count: int32 [4, 8, 2], P('axial', 'cross'), may hold values from 0 to 64, as said below
Outputs:
- velocity: float32 [4, 8, 8, 3, 128], P('axial', 'cross')
- residual: float32 [4, 8, 8, 3, 128], P('axial', 'cross')
- arrivals: float32 [4, 8, 3, 128], P('axial', 'cross')
Inputs may be any that keep to these rules, and one draw needn't show every extreme that they name: `tile_ids`: each entry is p * 8 + q with p one of 1, 3, 4, 5, 7 and q below 8; the first five tiles of every block name the five values of p. `mig_rows`: the 128 entries of one device are distinct beads. `mig_count`: the lowest slab sends nothing to the lower side and the highest nothing to the upper side; in every axial group one slab sends 64 beads to both sides.
All inputs are finite; a program needn't handle non-finite values.
Results may differ from a plain program's by a relative error of at most 0.024.
Values may be sent and summed in bfloat16 or wider, within the bound.
A program may use at most 64 MiB of HBM per device.

v0:
```python
import jax
import jax.numpy as jnp
from jax import lax
from jax.sharding import PartitionSpec as P

ITERS = 3


def padded(cells, sides, width, closed):
    for axis, dim in sides:
        count = lax.axis_size(axis)
        ends = count if closed else count - 1
        head = lax.slice_in_dim(cells, 0, width, axis=dim)
        tail = lax.slice_in_dim(cells, cells.shape[dim] - width, cells.shape[dim], axis=dim)
        cells = jnp.concatenate(
            [
                lax.ppermute(tail, axis, [(i, (i + 1) % count) for i in range(ends)]),
                cells,
                lax.ppermute(head, axis, [((i + 1) % count, i) for i in range(ends)]),
            ],
            axis=dim,
        )
    return cells


def passed_along(shard, axis, by):
    devices = lax.axis_size(axis)
    return lax.ppermute(shard, axis, [(i, (i + by) % devices) for i in range(devices)])


def shifted(shard, axis, by):
    devices = lax.axis_size(axis)
    pairs = [(i, i + by) for i in range(devices) if 0 <= i + by < devices]
    return lax.ppermute(shard, axis, pairs)


def neighbour_blocks(lowered):
    centre = lowered[0, 0]
    blanks = jnp.zeros_like(centre)
    axial_pad = padded(lowered, (("axial", 0),), 1, True)
    cross_pad = padded(lowered, (("cross", 1),), 1, False)
    below_axial = axial_pad[0, 0]
    above_axial = axial_pad[2, 0]
    below_cross = cross_pad[0, 0]
    above_cross = cross_pad[0, 2]
    return jnp.concatenate(
        [
            blanks,
            below_axial,
            blanks,
            below_cross,
            centre,
            above_cross,
            blanks,
            above_axial,
            blanks,
        ],
        axis=0,
    )


def apply_operator(direction, self_drag, tiles, tile_ids):
    blocks = tiles.shape[2]
    count = tiles.shape[3]
    width = tiles.shape[4]
    lowered = direction.astype(jnp.bfloat16)
    extended = neighbour_blocks(lowered)
    indices = tile_ids[0, 0].reshape(-1)
    own_tiles = tiles[0, 0]
    entries = lax.broadcasted_iota(jnp.int32, (blocks * count, 9 * blocks), 1)
    selector = entries == indices[:, None]
    picked = jnp.dot(
        selector.astype(jnp.bfloat16),
        extended.reshape(9 * blocks, 3 * width),
        preferred_element_type=jnp.float32,
    )
    picked = picked.astype(jnp.bfloat16).reshape(blocks, count, 3, width)
    coupled = jnp.einsum("bkij,bkcj->bci", own_tiles, picked, preferred_element_type=jnp.float32)
    coupled_low = coupled.astype(jnp.bfloat16)
    spread = jnp.einsum(
        "bkij,bci->bkcj", own_tiles, coupled_low, preferred_element_type=jnp.float32
    )
    summed = jnp.dot(
        selector.astype(jnp.float32).T,
        spread.reshape(blocks * count, 3 * width),
        precision=lax.Precision.HIGHEST,
        preferred_element_type=jnp.float32,
    )
    returned = summed.reshape(9, blocks, 3, width)
    from_upper_axial = passed_along(returned[1], "axial", -1)
    from_lower_axial = passed_along(returned[7], "axial", 1)
    from_upper_cross = shifted(returned[3], "cross", -1)
    from_lower_cross = shifted(returned[5], "cross", 1)
    total = returned[4] + from_upper_axial + from_lower_axial + from_upper_cross + from_lower_cross
    return self_drag[:, :, :, None, :] * direction + total[None, None]


def residual_squares(residual):
    return lax.psum(jnp.sum(residual * residual), ("axial", "cross"))


def on_device(force, self_drag, tiles, tile_ids, mig_rows, mig_count):
    velocity = jnp.zeros_like(force)
    residual = force
    direction = force
    norm_now = residual_squares(residual)
    for sweep in range(ITERS):
        image = apply_operator(direction, self_drag, tiles, tile_ids)
        alpha = norm_now / lax.psum(jnp.sum(direction * image), ("axial", "cross"))
        velocity = velocity + alpha * direction
        residual = residual - alpha * image
        norm_next = residual_squares(residual)
        direction = residual + norm_next / norm_now * direction
        norm_now = norm_next
    blocks = velocity.shape[2]
    width = velocity.shape[4]
    capacity = mig_rows.shape[3]
    flat = jnp.swapaxes(velocity[0, 0], 0, 1).reshape(3, blocks * width)
    picked = flat[:, mig_rows[0, 0].reshape(-1)].reshape(3, 2, capacity)
    live = lax.broadcasted_iota(jnp.int32, (1, 2, capacity), 2) < mig_count[0, 0][None, :, None]
    outgoing = jnp.where(live, picked, jnp.zeros_like(picked))
    from_lower = shifted(outgoing[:, 1], "cross", 1)
    from_upper = shifted(outgoing[:, 0], "cross", -1)
    arrivals = jnp.concatenate([from_lower, from_upper], axis=1)[None, None]
    return (velocity, residual, arrivals)


def solution(mesh):
    placed = (
        P("axial", "cross", None, None, None),
        P("axial", "cross", None, None),
        P("axial", "cross", None, None, None, None),
        P("axial", "cross", None, None),
        P("axial", "cross", None, None),
        P("axial", "cross", None),
    )
    return jax.shard_map(
        on_device,
        mesh=mesh,
        in_specs=placed,
        out_specs=(
            P("axial", "cross", None, None, None),
            P("axial", "cross", None, None, None),
            P("axial", "cross", None, None),
        ),
        check_vma=False,
    )
```

profile of v0, /device:TPU:0, one launch (start us, length us, event | category | flops | bytes accessed | tf_op | source)
XLA Modules:
  0.0 292.4 jit_solution(15793379436129139339)
XLA Ops:
  0.6 0.9 convert_element_type.33
  1.5 2.9 %collective-permute-start = (bf16[1,1,8,3,128]{4,2,3,1,0:T(8,128)(2,1)S(1)}, bf16[1,1,8,3,128]{4,2,3,1,0:T(8,128)(2,1)S(1)}, u32[]{:S(2)}, u32[]{:S(2)}) collective-permute-start(bf16[1,1,8,3,128]{4,2,3,1,0:T(8,128)(2,1)S(1)} %convert_element_type.33), channel_id=1, source_target_pairs={{0,8},{8,16},{16,24},{24,0},{1,9},{9,17},{17,25},{25,1},{2,10},{10... | collective-permute-start | bytes 18440 | tf_op jit(solution)/shard_map/ppermute | solution.py:17
  4.4 1.4 collective-permute-start.1
  5.9 1.3 collective-permute-start.2
  7.2 1.3 collective-permute-start.3
  8.5 0.8 eq.6
  9.3 0.7 constant_dynamic-update-slice_fusion.4
  11.2 0.9 fusion.12
  12.4 4.0 %collective-permute-start.7 = (f32[8,3,128]{2,0,1:T(8,128)S(1)}, f32[8,3,128]{2,0,1:T(8,128)S(1)}, u32[]{:S(2)}, u32[]{:S(2)}) collective-permute-start(f32[8,3,128]{2,0,1:T(8,128)S(1)} %get-tuple-element.27), channel_id=1, source_target_pairs={{0,1},{1,2},{2,3},{3,4},{4,5},{5,6},{6,7},{8,9},{9,10},{10,11},{11... | collective-permute-start | bytes 36872 | tf_op jit(solution)/shard_map/ppermute | solution.py:34
  16.5 1.3 collective-permute-start.6
  17.8 1.9 collective-permute-start.5
  19.7 1.0 collective-permute-start.4
  21.4 1.0 collective-permute-done.5
  22.4 1.0 collective-permute-done.4
  24.0 43.4 %all-reduce = (f32[]{:T(128)}, f32[]{:T(128)}) all-reduce(f32[]{:T(128)} %get-tuple-element.4, f32[]{:T(128)} %get-tuple-element.3), channel_id=1, replica_groups=mesh['axial'=4,'cross'=8] {'axial','cross'}, use_global_device_ids=true, to_apply=%region_1.0 | all-reduce | flops 2 | bytes 16 | tf_op jit(solution)/shard_map/psum | solution.py:99
  69.3 41.4 %psum.44 = f32[]{:T(128)} all-reduce(f32[]{:T(128)} %multiply_reduce_fusion.3), channel_id=1, replica_groups=mesh['axial'=4,'cross'=8] {'axial','cross'}, use_global_device_ids=true, to_apply=%region_5.0 | all-reduce | flops 1 | bytes 8 | tf_op jit(solution)/shard_map/psum | solution.py:99
  112.0 2.3 collective-permute-start.8
  114.4 1.3 collective-permute-start.9
  115.7 1.3 collective-permute-start.10
  117.0 0.7 collective-permute-start.11
  117.7 1.8 collective-permute-done.10
  119.5 1.1 collective-permute-done.11
  120.9 0.9 fusion.15
  122.2 3.2 %collective-permute-start.15 = (f32[8,3,128]{2,0,1:T(8,128)S(1)}, f32[8,3,128]{2,0,1:T(8,128)S(1)}, u32[]{:S(2)}, u32[]{:S(2)}) collective-permute-start(f32[8,3,128]{2,0,1:T(8,128)S(1)} %get-tuple-element.23), channel_id=1, source_target_pairs={{0,1},{1,2},{2,3},{3,4},{4,5},{5,6},{6,7},{8,9},{9,10},{10,11},{11... | collective-permute-start | bytes 36872 | tf_op jit(solution)/shard_map/ppermute | solution.py:34
  125.3 1.3 collective-permute-start.14
  126.6 2.1 collective-permute-start.13
  128.7 0.9 collective-permute-start.12
  130.3 1.0 collective-permute-done.13
  131.3 1.1 collective-permute-done.12
  133.0 43.0 %psum.45 = f32[]{:T(128)} all-reduce(f32[]{:T(128)} %get-tuple-element.13), channel_id=1, replica_groups=mesh['axial'=4,'cross'=8] {'axial','cross'}, use_global_device_ids=true, to_apply=%region_7.0 | all-reduce | flops 1 | bytes 8 | tf_op jit(solution)/shard_map/psum | solution.py:109
  178.0 40.9 %psum.46 = f32[]{:T(128)} all-reduce(f32[]{:T(128)} %get-tuple-element.11), channel_id=1, replica_groups=mesh['axial'=4,'cross'=8] {'axial','cross'}, use_global_device_ids=true, to_apply=%region_9.0 | all-reduce | flops 1 | bytes 8 | tf_op jit(solution)/shard_map/psum | solution.py:99
  220.3 2.3 collective-permute-start.16
  222.6 1.3 collective-permute-start.17
  223.9 1.3 collective-permute-start.18
  225.2 0.8 collective-permute-start.19
  226.0 1.7 collective-permute-done.18
  227.7 1.2 collective-permute-done.19
  229.1 0.9 fusion.18
  230.4 3.1 %collective-permute-start.23 = (f32[8,3,128]{2,0,1:T(8,128)S(1)}, f32[8,3,128]{2,0,1:T(8,128)S(1)}, u32[]{:S(2)}, u32[]{:S(2)}) collective-permute-start(f32[8,3,128]{2,0,1:T(8,128)S(1)} %get-tuple-element.19), channel_id=1, source_target_pairs={{0,1},{1,2},{2,3},{3,4},{4,5},{5,6},{6,7},{8,9},{9,10},{10,11},{11... | collective-permute-start | bytes 36872 | tf_op jit(solution)/shard_map/ppermute | solution.py:34
  233.5 1.3 collective-permute-start.22
  234.8 2.1 collective-permute-start.21
  236.9 0.9 collective-permute-start.20
  237.8 0.7 collective-permute-done.22
  238.5 1.0 collective-permute-done.21
  239.5 1.1 collective-permute-done.20
  241.2 43.0 %psum.47 = f32[]{:T(128)} all-reduce(f32[]{:T(128)} %get-tuple-element.7), channel_id=1, replica_groups=mesh['axial'=4,'cross'=8] {'axial','cross'}, use_global_device_ids=true, to_apply=%region_11.0 | all-reduce | flops 1 | bytes 8 | tf_op jit(solution)/shard_map/psum | solution.py:109
  286.6 1.3 collective-permute-start.25
  287.9 3.0 %collective-permute-start.24 = (f32[3,64]{1,0:T(4,128)S(1)}, f32[3,64]{1,0:T(4,128)S(1)}, u32[]{:S(2)}, u32[]{:S(2)}) collective-permute-start(f32[3,64]{1,0:T(4,128)S(1)} %get-tuple-element.30), channel_id=1, source_target_pairs={{0,1},{1,2},{2,3},{3,4},{4,5},{5,6},{6,7},{8,9},{9,10},{10,11},{11... | collective-permute-start | bytes 2312 | tf_op jit(solution)/shard_map/ppermute | solution.py:34
  (82 shorter events, 9.5 us)
Async XLA Ops:
  0.6 10.5 %copy-start = (bf16[1,1,8,8,128,128]{5,4,3,2,1,0:T(8,128)(2,1)S(1)}, bf16[1,1,8,8,128,128]{5,4,3,2,1,0:T(8,128)(2,1)}, u32[]{:S(2)}) copy-start(bf16[1,1,8,8,128,128]{5,4,3,2,1,0:T(8,128)(2,1)} %param.8) | copy-start | bytes 6291460
  1.5 7.8 %collective-permute-start = (bf16[1,1,8,3,128]{4,2,3,1,0:T(8,128)(2,1)S(1)}, bf16[1,1,8,3,128]{4,2,3,1,0:T(8,128)(2,1)S(1)}, u32[]{:S(2)}, u32[]{:S(2)}) collective-permute-start(bf16[1,1,8,3,128]{4,2,3,1,0:T(8,128)(2,1)S(1)} %convert_element_type.33), channel_id=1, source_target_pairs={{0,8},{8,16},{16,24},{24,0},{1,9},{9,17},{17,25},{25,1},{2,10},{10... | collective-permute-start | bytes 18440 | tf_op jit(solution)/shard_map/ppermute | solution.py:17
  4.4 4.8 %collective-permute-start.1 = (bf16[1,1,8,3,128]{4,2,3,1,0:T(8,128)(2,1)S(1)}, bf16[1,1,8,3,128]{4,2,3,1,0:T(8,128)(2,1)S(1)}, u32[]{:S(2)}, u32[]{:S(2)}) collective-permute-start(bf16[1,1,8,3,128]{4,2,3,1,0:T(8,128)(2,1)S(1)} %convert_element_type.33), channel_id=1, source_target_pairs={{0,1},{1,2},{2,3},{3,4},{4,5},{5,6},{6,7},{8,9},{9,10},{10,11},{11... | collective-permute-start | bytes 18440 | tf_op jit(solution)/shard_map/ppermute | solution.py:17
  5.9 4.7 %collective-permute-start.2 = (bf16[1,1,8,3,128]{4,2,3,1,0:T(8,128)(2,1)S(1)}, bf16[1,1,8,3,128]{4,2,3,1,0:T(8,128)(2,1)S(1)}, u32[]{:S(2)}, u32[]{:S(2)}) collective-permute-start(bf16[1,1,8,3,128]{4,2,3,1,0:T(8,128)(2,1)S(1)} %convert_element_type.33), channel_id=1, source_target_pairs={{1,0},{2,1},{3,2},{4,3},{5,4},{6,5},{7,6},{9,8},{10,9},{11,10},{12... | collective-permute-start | bytes 18440 | tf_op jit(solution)/shard_map/ppermute | solution.py:19
  7.2 3.7 %collective-permute-start.3 = (bf16[1,1,8,3,128]{4,2,3,1,0:T(8,128)(2,1)S(1)}, bf16[1,1,8,3,128]{4,2,3,1,0:T(8,128)(2,1)S(1)}, u32[]{:S(2)}, u32[]{:S(2)}) collective-permute-start(bf16[1,1,8,3,128]{4,2,3,1,0:T(8,128)(2,1)S(1)} %convert_element_type.33), channel_id=1, source_target_pairs={{8,0},{16,8},{24,16},{0,24},{9,1},{17,9},{25,17},{1,25},{10,2},{18... | collective-permute-start | bytes 18440 | tf_op jit(solution)/shard_map/ppermute | solution.py:19
  11.1 9.6 %copy-start.4 = (s32[1,1,2,64]{3,2,1,0:T(2,128)S(1)}, s32[1,1,2,64]{3,2,1,0:T(2,128)}, u32[]{:S(2)}) copy-start(s32[1,1,2,64]{3,2,1,0:T(2,128)} %param.10) | copy-start | bytes 1540
  11.1 12.3 %copy-start.1 = (f32[1,1,8,3,128]{4,2,3,1,0:T(8,128)S(1)}, f32[1,1,8,3,128]{4,2,3,1,0:T(8,128)}, u32[]{:S(2)}) copy-start(f32[1,1,8,3,128]{4,2,3,1,0:T(8,128)} %param.6) | copy-start | bytes 36868
  11.1 12.3 %copy-start.3 = (f32[1,1,8,128]{3,2,1,0:T(8,128)S(1)}, f32[1,1,8,128]{3,2,1,0:T(8,128)}, u32[]{:S(2)}) copy-start(f32[1,1,8,128]{3,2,1,0:T(8,128)} %param.7) | copy-start | bytes 12292
  12.4 8.4 %collective-permute-start.7 = (f32[8,3,128]{2,0,1:T(8,128)S(1)}, f32[8,3,128]{2,0,1:T(8,128)S(1)}, u32[]{:S(2)}, u32[]{:S(2)}) collective-permute-start(f32[8,3,128]{2,0,1:T(8,128)S(1)} %get-tuple-element.27), channel_id=1, source_target_pairs={{0,1},{1,2},{2,3},{3,4},{4,5},{5,6},{6,7},{8,9},{9,10},{10,11},{11... | collective-permute-start | bytes 36872 | tf_op jit(solution)/shard_map/ppermute | solution.py:34
  16.5 5.0 %collective-permute-start.6 = (f32[8,3,128]{2,0,1:T(8,128)S(1)}, f32[8,3,128]{2,0,1:T(8,128)S(1)}, u32[]{:S(2)}, u32[]{:S(2)}) collective-permute-start(f32[8,3,128]{2,0,1:T(8,128)S(1)} %get-tuple-element.28), channel_id=1, source_target_pairs={{1,0},{2,1},{3,2},{4,3},{5,4},{6,5},{7,6},{9,8},{10,9},{11,10},{12... | collective-permute-start | bytes 36872 | tf_op jit(solution)/shard_map/ppermute | solution.py:34
  17.8 4.6 %collective-permute-start.5 = (f32[8,3,128]{2,0,1:T(8,128)S(1)}, f32[8,3,128]{2,0,1:T(8,128)S(1)}, u32[]{:S(2)}, u32[]{:S(2)}) collective-permute-start(f32[8,3,128]{2,0,1:T(8,128)S(1)} %get-tuple-element.29), channel_id=1, source_target_pairs={{0,8},{8,16},{16,24},{24,0},{1,9},{9,17},{17,25},{25,1},{2,10},{10... | collective-permute-start | bytes 36872 | tf_op jit(solution)/shard_map/ppermute | solution.py:28
  19.7 3.7 %collective-permute-start.4 = (f32[8,3,128]{2,0,1:T(8,128)S(1)}, f32[8,3,128]{2,0,1:T(8,128)S(1)}, u32[]{:S(2)}, u32[]{:S(2)}) collective-permute-start(f32[8,3,128]{2,0,1:T(8,128)S(1)} %get-tuple-element.26), channel_id=1, source_target_pairs={{0,24},{8,0},{16,8},{24,16},{1,25},{9,1},{17,9},{25,17},{2,26},{10... | collective-permute-start | bytes 36872 | tf_op jit(solution)/shard_map/ppermute | solution.py:28
  112.0 5.6 %collective-permute-start.8 = (bf16[1,1,8,3,128]{4,2,3,1,0:T(8,128)(2,1)S(1)}, bf16[1,1,8,3,128]{4,2,3,1,0:T(8,128)(2,1)S(1)}, u32[]{:S(2)}, u32[]{:S(2)}) collective-permute-start(bf16[1,1,8,3,128]{4,2,3,1,0:T(8,128)(2,1)S(1)} %get-tuple-element.15), channel_id=1, source_target_pairs={{0,8},{8,16},{16,24},{24,0},{1,9},{9,17},{17,25},{25,1},{2,10},{10... | collective-permute-start | bytes 18440 | tf_op jit(solution)/shard_map/ppermute | solution.py:17
  114.4 3.3 %collective-permute-start.9 = (bf16[1,1,8,3,128]{4,2,3,1,0:T(8,128)(2,1)S(1)}, bf16[1,1,8,3,128]{4,2,3,1,0:T(8,128)(2,1)S(1)}, u32[]{:S(2)}, u32[]{:S(2)}) collective-permute-start(bf16[1,1,8,3,128]{4,2,3,1,0:T(8,128)(2,1)S(1)} %get-tuple-element.15), channel_id=1, source_target_pairs={{0,1},{1,2},{2,3},{3,4},{4,5},{5,6},{6,7},{8,9},{9,10},{10,11},{11... | collective-permute-start | bytes 18440 | tf_op jit(solution)/shard_map/ppermute | solution.py:17
  115.7 3.8 %collective-permute-start.10 = (bf16[1,1,8,3,128]{4,2,3,1,0:T(8,128)(2,1)S(1)}, bf16[1,1,8,3,128]{4,2,3,1,0:T(8,128)(2,1)S(1)}, u32[]{:S(2)}, u32[]{:S(2)}) collective-permute-start(bf16[1,1,8,3,128]{4,2,3,1,0:T(8,128)(2,1)S(1)} %get-tuple-element.15), channel_id=1, source_target_pairs={{1,0},{2,1},{3,2},{4,3},{5,4},{6,5},{7,6},{9,8},{10,9},{11,10},{12... | collective-permute-start | bytes 18440 | tf_op jit(solution)/shard_map/ppermute | solution.py:19
  117.0 3.7 %collective-permute-start.11 = (bf16[1,1,8,3,128]{4,2,3,1,0:T(8,128)(2,1)S(1)}, bf16[1,1,8,3,128]{4,2,3,1,0:T(8,128)(2,1)S(1)}, u32[]{:S(2)}, u32[]{:S(2)}) collective-permute-start(bf16[1,1,8,3,128]{4,2,3,1,0:T(8,128)(2,1)S(1)} %get-tuple-element.15), channel_id=1, source_target_pairs={{8,0},{16,8},{24,16},{0,24},{9,1},{17,9},{25,17},{1,25},{10,2},{18... | collective-permute-start | bytes 18440 | tf_op jit(solution)/shard_map/ppermute | solution.py:19
  120.9 8.8 %copy-start.5 = (s32[1,1,2]{2,1,0:T(1,128)S(1)}, s32[1,1,2]{2,1,0:T(1,128)}, u32[]{:S(2)}) copy-start(s32[1,1,2]{2,1,0:T(1,128)} %param.11) | copy-start | bytes 28
  122.2 7.5 %collective-permute-start.15 = (f32[8,3,128]{2,0,1:T(8,128)S(1)}, f32[8,3,128]{2,0,1:T(8,128)S(1)}, u32[]{:S(2)}, u32[]{:S(2)}) collective-permute-start(f32[8,3,128]{2,0,1:T(8,128)S(1)} %get-tuple-element.23), channel_id=1, source_target_pairs={{0,1},{1,2},{2,3},{3,4},{4,5},{5,6},{6,7},{8,9},{9,10},{10,11},{11... | collective-permute-start | bytes 36872 | tf_op jit(solution)/shard_map/ppermute | solution.py:34
  125.3 5.0 %collective-permute-start.14 = (f32[8,3,128]{2,0,1:T(8,128)S(1)}, f32[8,3,128]{2,0,1:T(8,128)S(1)}, u32[]{:S(2)}, u32[]{:S(2)}) collective-permute-start(f32[8,3,128]{2,0,1:T(8,128)S(1)} %get-tuple-element.24), channel_id=1, source_target_pairs={{1,0},{2,1},{3,2},{4,3},{5,4},{6,5},{7,6},{9,8},{10,9},{11,10},{12... | collective-permute-start | bytes 36872 | tf_op jit(solution)/shard_map/ppermute | solution.py:34
  126.6 4.6 %collective-permute-start.13 = (f32[8,3,128]{2,0,1:T(8,128)S(1)}, f32[8,3,128]{2,0,1:T(8,128)S(1)}, u32[]{:S(2)}, u32[]{:S(2)}) collective-permute-start(f32[8,3,128]{2,0,1:T(8,128)S(1)} %get-tuple-element.25), channel_id=1, source_target_pairs={{0,8},{8,16},{16,24},{24,0},{1,9},{9,17},{17,25},{25,1},{2,10},{10... | collective-permute-start | bytes 36872 | tf_op jit(solution)/shard_map/ppermute | solution.py:28
  128.7 3.7 %collective-permute-start.12 = (f32[8,3,128]{2,0,1:T(8,128)S(1)}, f32[8,3,128]{2,0,1:T(8,128)S(1)}, u32[]{:S(2)}, u32[]{:S(2)}) collective-permute-start(f32[8,3,128]{2,0,1:T(8,128)S(1)} %get-tuple-element.22), channel_id=1, source_target_pairs={{0,24},{8,0},{16,8},{24,16},{1,25},{9,1},{17,9},{25,17},{2,26},{10... | collective-permute-start | bytes 36872 | tf_op jit(solution)/shard_map/ppermute | solution.py:28
  220.3 5.7 %collective-permute-start.16 = (bf16[1,1,8,3,128]{4,2,3,1,0:T(8,128)(2,1)S(1)}, bf16[1,1,8,3,128]{4,2,3,1,0:T(8,128)(2,1)S(1)}, u32[]{:S(2)}, u32[]{:S(2)}) collective-permute-start(bf16[1,1,8,3,128]{4,2,3,1,0:T(8,128)(2,1)S(1)} %get-tuple-element.9), channel_id=1, source_target_pairs={{0,8},{8,16},{16,24},{24,0},{1,9},{9,17},{17,25},{25,1},{2,10},{10... | collective-permute-start | bytes 18440 | tf_op jit(solution)/shard_map/ppermute | solution.py:17
  222.6 3.4 %collective-permute-start.17 = (bf16[1,1,8,3,128]{4,2,3,1,0:T(8,128)(2,1)S(1)}, bf16[1,1,8,3,128]{4,2,3,1,0:T(8,128)(2,1)S(1)}, u32[]{:S(2)}, u32[]{:S(2)}) collective-permute-start(bf16[1,1,8,3,128]{4,2,3,1,0:T(8,128)(2,1)S(1)} %get-tuple-element.9), channel_id=1, source_target_pairs={{0,1},{1,2},{2,3},{3,4},{4,5},{5,6},{6,7},{8,9},{9,10},{10,11},{11... | collective-permute-start | bytes 18440 | tf_op jit(solution)/shard_map/ppermute | solution.py:17
  223.9 3.8 %collective-permute-start.18 = (bf16[1,1,8,3,128]{4,2,3,1,0:T(8,128)(2,1)S(1)}, bf16[1,1,8,3,128]{4,2,3,1,0:T(8,128)(2,1)S(1)}, u32[]{:S(2)}, u32[]{:S(2)}) collective-permute-start(bf16[1,1,8,3,128]{4,2,3,1,0:T(8,128)(2,1)S(1)} %get-tuple-element.9), channel_id=1, source_target_pairs={{1,0},{2,1},{3,2},{4,3},{5,4},{6,5},{7,6},{9,8},{10,9},{11,10},{12... | collective-permute-start | bytes 18440 | tf_op jit(solution)/shard_map/ppermute | solution.py:19
  225.2 3.7 %collective-permute-start.19 = (bf16[1,1,8,3,128]{4,2,3,1,0:T(8,128)(2,1)S(1)}, bf16[1,1,8,3,128]{4,2,3,1,0:T(8,128)(2,1)S(1)}, u32[]{:S(2)}, u32[]{:S(2)}) collective-permute-start(bf16[1,1,8,3,128]{4,2,3,1,0:T(8,128)(2,1)S(1)} %get-tuple-element.9), channel_id=1, source_target_pairs={{8,0},{16,8},{24,16},{0,24},{9,1},{17,9},{25,17},{1,25},{10,2},{18... | collective-permute-start | bytes 18440 | tf_op jit(solution)/shard_map/ppermute | solution.py:19
  230.4 7.4 %collective-permute-start.23 = (f32[8,3,128]{2,0,1:T(8,128)S(1)}, f32[8,3,128]{2,0,1:T(8,128)S(1)}, u32[]{:S(2)}, u32[]{:S(2)}) collective-permute-start(f32[8,3,128]{2,0,1:T(8,128)S(1)} %get-tuple-element.19), channel_id=1, source_target_pairs={{0,1},{1,2},{2,3},{3,4},{4,5},{5,6},{6,7},{8,9},{9,10},{10,11},{11... | collective-permute-start | bytes 36872 | tf_op jit(solution)/shard_map/ppermute | solution.py:34
  233.5 4.9 %collective-permute-start.22 = (f32[8,3,128]{2,0,1:T(8,128)S(1)}, f32[8,3,128]{2,0,1:T(8,128)S(1)}, u32[]{:S(2)}, u32[]{:S(2)}) collective-permute-start(f32[8,3,128]{2,0,1:T(8,128)S(1)} %get-tuple-element.20), channel_id=1, source_target_pairs={{1,0},{2,1},{3,2},{4,3},{5,4},{6,5},{7,6},{9,8},{10,9},{11,10},{12... | collective-permute-start | bytes 36872 | tf_op jit(solution)/shard_map/ppermute | solution.py:34
  234.8 4.6 %collective-permute-start.21 = (f32[8,3,128]{2,0,1:T(8,128)S(1)}, f32[8,3,128]{2,0,1:T(8,128)S(1)}, u32[]{:S(2)}, u32[]{:S(2)}) collective-permute-start(f32[8,3,128]{2,0,1:T(8,128)S(1)} %get-tuple-element.21), channel_id=1, source_target_pairs={{0,8},{8,16},{16,24},{24,0},{1,9},{9,17},{17,25},{25,1},{2,10},{10... | collective-permute-start | bytes 36872 | tf_op jit(solution)/shard_map/ppermute | solution.py:28
  236.9 3.7 %collective-permute-start.20 = (f32[8,3,128]{2,0,1:T(8,128)S(1)}, f32[8,3,128]{2,0,1:T(8,128)S(1)}, u32[]{:S(2)}, u32[]{:S(2)}) collective-permute-start(f32[8,3,128]{2,0,1:T(8,128)S(1)} %get-tuple-element.18), channel_id=1, source_target_pairs={{0,24},{8,0},{16,8},{24,16},{1,25},{9,1},{17,9},{25,17},{2,26},{10... | collective-permute-start | bytes 36872 | tf_op jit(solution)/shard_map/ppermute | solution.py:28
  285.6 6.8 %copy-start.2 = (f32[1,1,8,3,128]{4,2,3,1,0:T(8,128)}, f32[1,1,8,3,128]{4,2,3,1,0:T(8,128)S(1)}, u32[]{:S(2)}) copy-start(f32[1,1,8,3,128]{4,2,3,1,0:T(8,128)S(1)} %multiply_add_fusion) | copy-start | bytes 36868
  286.6 4.9 %collective-permute-start.25 = (f32[3,64]{1,0:T(4,128)S(1)}, f32[3,64]{1,0:T(4,128)S(1)}, u32[]{:S(2)}, u32[]{:S(2)}) collective-permute-start(f32[3,64]{1,0:T(4,128)S(1)} %get-tuple-element.31), channel_id=1, source_target_pairs={{1,0},{2,1},{3,2},{4,3},{5,4},{6,5},{7,6},{9,8},{10,9},{11,10},{12... | collective-permute-start | bytes 2312 | tf_op jit(solution)/shard_map/ppermute | solution.py:34
  287.9 3.8 %collective-permute-start.24 = (f32[3,64]{1,0:T(4,128)S(1)}, f32[3,64]{1,0:T(4,128)S(1)}, u32[]{:S(2)}, u32[]{:S(2)}) collective-permute-start(f32[3,64]{1,0:T(4,128)S(1)} %get-tuple-element.30), channel_id=1, source_target_pairs={{0,1},{1,2},{2,3},{3,4},{4,5},{5,6},{6,7},{8,9},{9,10},{10,11},{11... | collective-permute-start | bytes 2312 | tf_op jit(solution)/shard_map/ppermute | solution.py:34
where the time goes:
time: 295 us; the launch traced here: 292 us
  blocking collectives  212 us (72%)
  starting transfers between devices  45.7 us (15%)
  waiting for transfers between devices  14.9 us (5%)
  between operations  7.67 us (3%)
  other arithmetic  5.41 us (2%)
  matrix products  4.37 us (1%)
    psum x3, blocking collectives, residual_squares(): return lax.psum(jnp.sum(residual * residual), ('axial', 'cross'))  126 us
    psum x2, blocking collectives, on_device(): alpha = norm_now / lax.psum(jnp.sum(direction * image), ('axial', 'cross'))  86.1 us
    ppermute x8, starting transfers between devices, shifted(): return lax.ppermute(shard, axis, pairs)  18.5 us
    ppermute x6, starting transfers between devices, padded(): lax.ppermute(tail, axis, [(i, (i + 1) % count) for i in range(ends)])  11.6 us
    ppermute x6, starting transfers between devices, passed_along(): lax.ppermute(shard, axis, [(i, (i + by) % devices) for i in range(devices)])  8.93 us
    ppermute x6, starting transfers between devices, padded(): lax.ppermute(head, axis, [((i + 1) % count, i) for i in range(ends)])  6.64 us
    ppermute x6, waiting for transfers between devices, padded(): lax.ppermute(head, axis, [((i + 1) % count, i) for i in range(ends)])  6.6 us
    ppermute x6, waiting for transfers between devices, passed_along(): lax.ppermute(shard, axis, [(i, (i + by) % devices) for i in range(devices)])  6.25 us
  transfers between devices with their start and end apart: 26, of which 16 were waited for; matrix products, arithmetic and copies ran while one was open for 1% of the time, Pallas kernels for 0%

commit v1 on v0

v1 whole, which is shorter than its diff:
```python
import functools

import jax
import jax.numpy as jnp
from jax import lax
from jax.experimental import pallas as pl
from jax.experimental.pallas import tpu as pltpu
from jax.sharding import PartitionSpec as P

ITERS = 3
MESH = pl.DeviceIdType.MESH
PLACES = (1, 3, 5, 7)
CENTRE = 4
F32 = jnp.float32
BF16 = jnp.bfloat16


def chunks(field):
    return [field[:, c * 128:(c + 1) * 128] for c in range(3)]


def kernel(
    n_ax, n_cr,
    ids_ref, count_ref, force_ref, drag_ref, tiles_ref, rows_ref,
    vel_ref, res_ref, arr_ref,
    tile_buf, ext, spread, own, halo, ret_out, ret_in, part_ax, part_cr, mig, rows_out, rows_in,
    tile_sem, halo_send, halo_recv, ret_send, ret_recv, rows_send, rows_recv,
    ax_send, ax_recv, cr_send, cr_recv,
):
    blocks, count, width = tiles_ref.shape[0], tiles_ref.shape[1], tiles_ref.shape[2]
    pairs = blocks * count
    slot = rows_ref.shape[1]
    me_a = lax.axis_index("axial")
    me_c = lax.axis_index("cross")

    def ax_peer(step):
        return {"axial": lax.rem(me_a + step, n_ax)}

    def cr_peer(step):
        return {"cross": lax.rem(me_c + step, n_cr)}

    device = (ax_peer(n_ax - 1), cr_peer(n_cr - 1), cr_peer(1), ax_peer(1))
    exists = (None, me_c > 0, me_c + 1 < n_cr, None)

    def guarded(d, act):
        if exists[d] is None:
            act()
        else:
            pl.when(exists[d])(act)

    def neighbour(src, dst, send, recv, d, back):
        s = d if back else 3 - d
        return pltpu.make_async_remote_copy(
            src_ref=src, dst_ref=dst.at[s], send_sem=send.at[d], recv_sem=recv.at[s],
            device_id=device[d], device_id_type=MESH,
        )

    def halo_copy(stage, d, back=False):
        return neighbour(own.at[stage], halo.at[stage], halo_send.at[stage], halo_recv.at[stage], d, back)

    def ret_copy(it, d, back=False):
        src = ret_out.at[it, pl.ds(PLACES[d] * blocks, blocks)]
        return neighbour(src, ret_in.at[it], ret_send.at[it], ret_recv.at[it], d, back)

    def rows_copy(d, back=False):
        return neighbour(rows_out.at[d], rows_in, rows_send, rows_recv, d, back)

    def ax_copy(it, step):
        return pltpu.make_async_remote_copy(
            src_ref=part_ax.at[it, me_a], dst_ref=part_ax.at[it, me_a],
            send_sem=ax_send.at[it, step], recv_sem=ax_recv.at[it, step],
            device_id=ax_peer(step), device_id_type=MESH,
        )

    def cr_copy(it, step):
        return pltpu.make_async_remote_copy(
            src_ref=part_cr.at[it, me_c], dst_ref=part_cr.at[it, me_c],
            send_sem=cr_send.at[it, step], recv_sem=cr_recv.at[it, step],
            device_id=cr_peer(step), device_id_type=MESH,
        )

    barrier = pltpu.get_barrier_semaphore()
    for step in range(1, n_ax):
        pl.semaphore_signal(barrier, inc=1, device_id=ax_peer(step), device_id_type=MESH)
    for step in range(1, n_cr):
        pl.semaphore_signal(barrier, inc=1, device_id=cr_peer(step), device_id_type=MESH)

    load = pltpu.make_async_copy(tiles_ref, tile_buf, tile_sem)
    load.start()

    force = jnp.concatenate([force_ref[c] for c in range(3)], axis=1)
    own[0] = force
    lane = lax.broadcasted_iota(jnp.int32, (1, 128), 1)
    mig[0:2, 0:slot] = rows_ref[...]
    listed = mig[...]
    turned = pltpu.roll(listed, 64, 1)
    rows_out[1] = jnp.where((lane < slot) & (lane < count_ref[0]), listed[0:1], -1)
    rows_out[2] = jnp.where((lane >= 64) & (lane - 64 < count_ref[1]), turned[1:2], -1)

    for d in (1, 2):
        @pl.when(jnp.logical_not(exists[d]))
        def _():
            for stage in range(ITERS):
                halo[stage, d] = jnp.zeros((blocks, 3 * width), F32)
                ret_in[stage, d] = jnp.zeros((blocks, 3 * width), F32)
            rows_in[d] = jnp.full((1, 128), -1, jnp.int32)

    pl.semaphore_wait(barrier, n_ax - 1 + n_cr - 1)

    for d in range(4):
        guarded(d, lambda d=d: halo_copy(0, d).start())
    for d in (1, 2):
        guarded(d, lambda d=d: rows_copy(d).start())

    ext[...] = jnp.zeros(ext.shape, F32)
    wide = lax.broadcasted_iota(jnp.int32, (1, 2 * pairs), 1)
    listed_ids = jnp.zeros((1, 2 * pairs), jnp.int32)
    for n in range(pairs):
        hit = (wide == n) | (wide == n + pairs)
        listed_ids = jnp.where(hit, ids_ref[n // count, n % count], listed_ids)
    entry = lax.broadcasted_iota(jnp.int32, (8 * blocks, 2 * pairs), 0)
    selector = jnp.where(entry == listed_ids, 1.0, 0.0).astype(BF16)
    drag = drag_ref[...]
    drag3 = jnp.concatenate([drag] * 3, axis=1)

    def place(p, field):
        for c, part in enumerate(chunks(field)):
            ext[p * blocks:(p + 1) * blocks, c, :] = part

    def tile_row(b):
        return jnp.concatenate([tile_buf[b, k] for k in range(count)], axis=1)

    def total(parts):
        return jnp.sum(functools.reduce(jnp.add, parts), axis=0, keepdims=True)

    place(CENTRE, force)
    residual = force
    velocity = direction = image = None
    near = [None] * 4
    near_image = [None] * 4
    near_velocity = [None] * 4
    near_direction = [None] * 4
    track = [None] * blocks
    norm_before = energy_before = None

    for d in range(4):
        guarded(d, lambda d=d: halo_copy(0, d, True).wait_recv())
        near[d] = halo[0, d]
    load.wait()

    for it in range(ITERS):
        last = it == ITERS - 1
        if it:
            place(CENTRE, residual)
        for d in range(4):
            place(PLACES[d], near[d])
        coupled = []
        for b in range(blocks):
            picked = jnp.concatenate([ext[ids_ref[b, k]] for k in range(count)], axis=1)
            coupled.append(lax.dot_general(
                picked.astype(BF16), tile_row(b), (((1,), (1,)), ((), ())), preferred_element_type=F32,
            ))

        square = functools.reduce(jnp.add, chunks(residual * residual))
        sums = [
            jnp.sum(square, axis=0, keepdims=True),
            total([drag * square] + [c * c for c in coupled]),
        ]
        if it:
            mixed = functools.reduce(jnp.add, chunks(residual * direction))
            sums.append(total([drag * mixed] + [c * t for c, t in zip(coupled, track)]))
        else:
            sums.append(jnp.zeros((1, 128), F32))
        part_ax[it, me_a] = jnp.concatenate(sums, axis=1)
        for step in range(1, n_ax):
            ax_copy(it, step).start()

        for b in range(blocks):
            back = jnp.dot(coupled[b].astype(BF16), tile_row(b), preferred_element_type=F32)
            for k in range(count):
                spread[b * count + k] = back[:, k * width:(k + 1) * width]
        listed_spread = jnp.concatenate([spread[:, c, :] for c in range(3)], axis=1)
        high = listed_spread.astype(BF16)
        low = (listed_spread - high.astype(F32)).astype(BF16)
        ret_out[it] = jnp.dot(
            selector, jnp.concatenate([high, low], axis=0), preferred_element_type=F32
        )
        for d in range(4):
            guarded(d, lambda d=d: ret_copy(it, d).start())

        for step in range(1, n_ax):
            ax_copy(it, step).wait_recv()
        part_cr[it, me_c] = functools.reduce(jnp.add, [part_ax[it, i] for i in range(n_ax)])
        for step in range(1, n_cr):
            cr_copy(it, step).start()

        if last:
            gathered = [0.0] * 9
            for d in (1, 2):
                if it == ITERS - 1:
                    guarded(d, lambda d=d: rows_copy(d, True).wait_recv())
                rows = rows_in[d]
                fields = [near_velocity[d], near[d], near_direction[d]]
                stack = jnp.concatenate([part for f in fields for part in chunks(f)], axis=0)
                first = stack.astype(BF16)
                rest = stack - first.astype(F32)
                second = rest.astype(BF16)
                third = (rest - second.astype(F32)).astype(BF16)
                bead = lax.broadcasted_iota(jnp.int32, (width, 128), 0)
                onehot = jnp.where(bead == (rows & (width - 1)), 1.0, 0.0).astype(BF16)
                found = sum(
                    jnp.dot(piece, onehot, preferred_element_type=F32) for piece in (third, second, first)
                )
                block = lax.broadcasted_iota(jnp.int32, (blocks, 128), 0)
                mine = block == (rows >> (width.bit_length() - 1))
                for n in range(9):
                    part = jnp.where(mine, found[n * blocks:(n + 1) * blocks], 0.0)
                    gathered[n] = gathered[n] + jnp.sum(part, axis=0, keepdims=True)

        for d in range(4):
            guarded(d, lambda d=d: ret_copy(it, d, True).wait_recv())
        product = drag3 * residual + ret_out[it, CENTRE * blocks:(CENTRE + 1) * blocks]
        for d in range(4):
            product = product + ret_in[it, d]
        if not last:
            own[it + 1] = product
            for d in range(4):
                guarded(d, lambda d=d: halo_copy(it + 1, d).start())

        for step in range(1, n_cr):
            cr_copy(it, step).wait_recv()
        summed = functools.reduce(jnp.add, [part_cr[it, i] for i in range(n_cr)])
        norm, energy, cross = [jnp.sum(s, axis=1, keepdims=True) for s in chunks(summed)]
        if it:
            beta = norm / norm_before
            energy = energy + 2.0 * beta * cross + beta * beta * energy_before
        alpha = norm / energy
        norm_before, energy_before = norm, energy

        def follow(now, before):
            return now + beta * before if it else now

        image = follow(product, image)
        direction = follow(residual, direction)
        velocity = velocity + alpha * direction if it else alpha * direction
        residual = residual - alpha * image
        if last:
            break
        track = [follow(c, t) for c, t in zip(coupled, track)]
        for d in range(4):
            guarded(d, lambda d=d: halo_copy(it + 1, d, True).wait_recv())
            near_image[d] = follow(halo[it + 1, d], near_image[d])
            if d in (1, 2):
                near_direction[d] = follow(near[d], near_direction[d])
                step_v = alpha * near_direction[d]
                near_velocity[d] = near_velocity[d] + step_v if it else step_v
            near[d] = near[d] - alpha * near_image[d]

    for c in range(3):
        vel_ref[c] = chunks(velocity)[c]
        res_ref[c] = chunks(residual)[c]
    sub = lax.broadcasted_iota(jnp.int32, (8, 128), 0)
    arrived = jnp.zeros((8, 128), F32)
    for c in range(3):
        row = gathered[c] + alpha * (gathered[3 + c] + beta * gathered[6 + c])
        arrived = jnp.where(sub == c, row, arrived)
    arr_ref[...] = pltpu.roll(arrived, 64, 1)[0:3]

    for d in (1, 2):
        guarded(d, lambda d=d: rows_copy(d).wait_send())
    for it in range(ITERS):
        for d in range(4):
            guarded(d, lambda d=d: halo_copy(it, d).wait_send())
            guarded(d, lambda d=d: ret_copy(it, d).wait_send())
        for step in range(1, n_ax):
            ax_copy(it, step).wait_send()
        for step in range(1, n_cr):
            cr_copy(it, step).wait_send()


def on_device(n_ax, n_cr, force, self_drag, tiles, tile_ids, mig_rows, mig_count):
    blocks, width = force.shape[2], force.shape[4]
    count = tiles.shape[3]
    field = (blocks, 3 * width)
    vmem = pl.BlockSpec(memory_space=pltpu.VMEM)
    smem = pl.BlockSpec(memory_space=pltpu.SMEM)
    dma = pltpu.SemaphoreType.DMA
    velocity, residual, arrivals = pl.pallas_call(
        functools.partial(kernel, n_ax, n_cr),
        out_shape=(
            jax.ShapeDtypeStruct((3, blocks, width), F32),
            jax.ShapeDtypeStruct((3, blocks, width), F32),
            jax.ShapeDtypeStruct((3, 2 * mig_rows.shape[3]), F32),
        ),
        in_specs=[smem, smem, vmem, vmem, pl.BlockSpec(memory_space=pl.ANY), vmem],
        out_specs=(vmem, vmem, vmem),
        scratch_shapes=[
            pltpu.VMEM((blocks, count, width, width), BF16),
            pltpu.VMEM((8 * blocks, 8, width), F32),
            pltpu.VMEM((blocks * count, 8, width), F32),
            pltpu.VMEM((ITERS,) + field, F32),
            pltpu.VMEM((ITERS, 4) + field, F32),
            pltpu.VMEM((ITERS, 8 * blocks, 3 * width), F32),
            pltpu.VMEM((ITERS, 4) + field, F32),
            pltpu.VMEM((ITERS, n_ax, 1, 384), F32),
            pltpu.VMEM((ITERS, n_cr, 1, 384), F32),
            pltpu.VMEM((8, 128), jnp.int32),
            pltpu.VMEM((3, 1, 128), jnp.int32),
            pltpu.VMEM((3, 1, 128), jnp.int32),
            dma,
            dma((ITERS, 4)), dma((ITERS, 4)),
            dma((ITERS, 4)), dma((ITERS, 4)),
            dma((3,)), dma((3,)),
            dma((ITERS, n_ax)), dma((ITERS, n_ax)),
            dma((ITERS, n_cr)), dma((ITERS, n_cr)),
        ],
        compiler_params=pltpu.CompilerParams(
            collective_id=0, has_side_effects=True, vmem_limit_bytes=60 * 1024 * 1024
        ),
        name="cg_solve",
    )(
        tile_ids.reshape(tile_ids.shape[2:]),
        mig_count.reshape(mig_count.shape[2:]),
        jnp.swapaxes(force[0, 0], 0, 1),
        self_drag.reshape(self_drag.shape[2:]),
        tiles.reshape(tiles.shape[2:]),
        mig_rows.reshape(mig_rows.shape[2:]),
    )
    velocity, residual = jnp.swapaxes(velocity, 0, 1), jnp.swapaxes(residual, 0, 1)
    return velocity[None, None], residual[None, None], arrivals[None, None]


def solution(mesh):
    placed = (
        P("axial", "cross", None, None, None),
        P("axial", "cross", None, None),
        P("axial", "cross", None, None, None, None),
        P("axial", "cross", None, None),
        P("axial", "cross", None, None),
        P("axial", "cross", None),
    )
    return jax.shard_map(
        functools.partial(on_device, mesh.shape["axial"], mesh.shape["cross"]),
        mesh=mesh,
        in_specs=placed,
        out_specs=(
            P("axial", "cross", None, None, None),
            P("axial", "cross", None, None, None),
            P("axial", "cross", None, None),
        ),
        check_vma=False,
    )
```

time: 295 us -> 39.3 us (0.13)
  blocking collectives: 212 us -> 0 us
  starting transfers between devices: 45.7 us -> 0 us
  Pallas kernels: 0 us -> 34.5 us
  waiting for transfers between devices: 14.9 us -> 0 us
  between operations: 7.67 us -> 0.64 us
  other arithmetic: 5.41 us -> 0 us
  matrix products: 4.37 us -> 0 us
    psum x5 -> x0, blocking collectives: 212 us -> none  [the longest x3 126 us: residual_squares(): return lax.psum(jnp.sum(residual * residual), ('axial', 'cross'))]
    ppermute x26 -> x0, starting transfers between devices: 45.7 us -> none  [the longest x8 18.5 us: shifted(): return lax.ppermute(shard, axis, pairs)]
    pallas_call x0 -> x1, Pallas kernels: none -> 34.5 us  [on_device(): pl.pallas_call(functools.partial(kernel, n_ax, n_cr), out_shape=(jax.Shap...]
    ppermute x26 -> x0, waiting for transfers between devices: 14.9 us -> none  [the longest x6 6.6 us: padded(): lax.ppermute(head, axis, [((i + 1) % count, i) for i in range(ends)])]
    dot_general x9 -> x0, matrix products: 4.37 us -> none  [the longest x3 2.78 us: apply_operator(): jnp.einsum('bkij,bci->bkcj', own_tiles, coupled_low, preferred_element_ty...]
    unnamed x35 -> x3, local copies, waits for them, and re-layouts: 0.2 us -> 3.84 us
    reduce_sum x5 -> x0, other arithmetic: 3.04 us -> none  [the longest x3 1.83 us: on_device(): alpha = norm_now / lax.psum(jnp.sum(direction * image), ('axial', 'cross'))]
  transfers between devices with their start and end apart: 26 -> 0, of which waited for: 16 -> 0; matrix products, arithmetic and copies ran while one was open for 1% -> 0% of each run, Pallas kernels for 0% -> 0%
where the time goes in v1:
time: 39.3 us; the launch traced here: 39 us
  Pallas kernels  34.5 us (88%)
  local copies, waits for them, and re-layouts  3.84 us (10%)
  between operations  0.64 us (2%)
    pallas_call x1, Pallas kernels, on_device(): pl.pallas_call(functools.partial(kernel, n_ax, n_cr), out_shape=(jax.Shap...  34.5 us
    unnamed x3, local copies, waits for them, and re-layouts  3.84 us

profile of v1, /device:TPU:0, one launch (start us, length us, event | category | flops | bytes accessed | tf_op | source)
XLA Modules:
  0.0 39.0 jit_solution(1278977404867825663)
XLA Ops:
  0.6 34.5 %cg_solve.1 = (f32[3,8,128]{2,1,0:T(8,128)}, f32[3,8,128]{2,1,0:T(8,128)}, f32[3,128]{1,0:T(4,128)}) custom-call(s32[8,8]{1,0:T(8,128)} %bitcast.19, s32[2]{0:T(128)} %bitcast.23, f32[3,8,128]{2,1,0:T(8,128)} %bitcast.16, f32[8,128]{1,0:T(8,128)} %bitcast.20, bf16[8,8,128,128]{3,2,1,0:T(8,128)(2,1)} %bitcast.15, s32[2,64]{1,0:T(2,128)} %bitcast.22), custom_call_target="tpu_custom_call" | custom-call | tf_op jit(solution)/shard_map/cg_solve/pallas_call | solution.py:288
  35.1 1.2 %copy.9 = f32[1,1,3,128]{3,1,2,0:T(1,128)} copy(f32[1,1,3,128]{3,2,1,0:T(4,128)} %bitcast.21) | data formatting | bytes 3072
  36.3 1.3 %copy.12 = f32[1,1,8,3,128]{4,2,3,1,0:T(8,128)} copy(f32[1,1,8,3,128]{4,2,3,1,0:T(8,128)} %bitcast.18) | data formatting | bytes 24576
  37.7 1.3 %copy.13 = f32[1,1,8,3,128]{4,2,3,1,0:T(8,128)} copy(f32[1,1,8,3,128]{4,2,3,1,0:T(8,128)} %bitcast.17) | data formatting | bytes 24576

commit v2 on v1

--- a/solution.py
+++ b/solution.py
@@ -21,15 +21,15 @@
 
 def kernel(
     n_ax, n_cr,
-    ids_ref, count_ref, force_ref, drag_ref, tiles_ref, rows_ref,
+    ids_hbm, count_hbm, force_hbm, drag_hbm, tiles_ref, rows_hbm,
     vel_ref, res_ref, arr_ref,
-    tile_buf, ext, spread, own, halo, ret_out, ret_in, part_ax, part_cr, mig, rows_out, rows_in,
-    tile_sem, halo_send, halo_recv, ret_send, ret_recv, rows_send, rows_recv,
+    ids_ref, count_ref, force_ref, drag_ref, rows_ref, tile_buf, ext, spread, own, halo, ret_out, ret_in, part_ax, part_cr, mig, rows_out, rows_in,
+    tile_sem, small_sem, halo_send, halo_recv, ret_send, ret_recv, rows_send, rows_recv,
     ax_send, ax_recv, cr_send, cr_recv,
 ):
     blocks, count, width = tiles_ref.shape[0], tiles_ref.shape[1], tiles_ref.shape[2]
     pairs = blocks * count
-    slot = rows_ref.shape[1]
+    slot = rows_hbm.shape[1]
     me_a = lax.axis_index("axial")
     me_c = lax.axis_index("cross")
 
@@ -48,36 +48,57 @@
         else:
             pl.when(exists[d])(act)
 
-    def neighbour(src, dst, send, recv, d, back):
-        s = d if back else 3 - d
+    def neighbour(src, dst, send, recv, d):
         return pltpu.make_async_remote_copy(
-            src_ref=src, dst_ref=dst.at[s], send_sem=send.at[d], recv_sem=recv.at[s],
+            src_ref=src, dst_ref=dst.at[3 - d], send_sem=send, recv_sem=recv,
             device_id=device[d], device_id_type=MESH,
         )
 
-    def halo_copy(stage, d, back=False):
-        return neighbour(own.at[stage], halo.at[stage], halo_send.at[stage], halo_recv.at[stage], d, back)
-
-    def ret_copy(it, d, back=False):
+    def halo_copy(stage, d):
+        return neighbour(own.at[stage], halo.at[stage], halo_send.at[d], halo_recv.at[stage], d)
+
+    def ret_copy(it, d):
         src = ret_out.at[it, pl.ds(PLACES[d] * blocks, blocks)]
-        return neighbour(src, ret_in.at[it], ret_send.at[it], ret_recv.at[it], d, back)
-
-    def rows_copy(d, back=False):
-        return neighbour(rows_out.at[d], rows_in, rows_send, rows_recv, d, back)
+        return neighbour(src, ret_in.at[it], ret_send.at[d], ret_recv.at[it], d)
+
+    def rows_copy(d):
+        return neighbour(rows_out.at[d], rows_in, rows_send.at[d], rows_recv.at[3 - d], d)
+
+    def wait_for(ref, sem):
+        pltpu.make_async_copy(ref, ref, sem).wait()
+
+    inner = exists[1] & exists[2]
+
+    def arrived_all(ref, sem):
+        @pl.when(inner)
+        def _():
+            wait_for(ref, sem)
+
+        @pl.when(jnp.logical_not(inner))
+        def _():
+            wait_for(ref.at[pl.ds(0, 3)], sem)
 
     def ax_copy(it, step):
         return pltpu.make_async_remote_copy(
             src_ref=part_ax.at[it, me_a], dst_ref=part_ax.at[it, me_a],
-            send_sem=ax_send.at[it, step], recv_sem=ax_recv.at[it, step],
+            send_sem=ax_send, recv_sem=ax_recv.at[it],
             device_id=ax_peer(step), device_id_type=MESH,
         )
 
     def cr_copy(it, step):
         return pltpu.make_async_remote_copy(
             src_ref=part_cr.at[it, me_c], dst_ref=part_cr.at[it, me_c],
-            send_sem=cr_send.at[it, step], recv_sem=cr_recv.at[it, step],
+            send_sem=cr_send, recv_sem=cr_recv.at[it],
             device_id=cr_peer(step), device_id_type=MESH,
         )
+
+    fetched = (
+        (force_hbm, force_ref), (ids_hbm, ids_ref), (count_hbm, count_ref),
+        (drag_hbm, drag_ref), (rows_hbm, rows_ref),
+    )
+    small = [pltpu.make_async_copy(a, b, small_sem.at[n]) for n, (a, b) in enumerate(fetched)]
+    for copy in small:
+        copy.start()
 
     barrier = pltpu.get_barrier_semaphore()
     for step in range(1, n_ax):
@@ -87,6 +108,8 @@
 
     load = pltpu.make_async_copy(tiles_ref, tile_buf, tile_sem)
     load.start()
+    for copy in small:
+        copy.wait()
 
     force = jnp.concatenate([force_ref[c] for c in range(3)], axis=1)
     own[0] = force
@@ -143,8 +166,8 @@
     track = [None] * blocks
     norm_before = energy_before = None
 
+    arrived_all(halo.at[0], halo_recv.at[0])
     for d in range(4):
-        guarded(d, lambda d=d: halo_copy(0, d, True).wait_recv())
         near[d] = halo[0, d]
     load.wait()
 
@@ -188,8 +211,7 @@
         for d in range(4):
             guarded(d, lambda d=d: ret_copy(it, d).start())
 
-        for step in range(1, n_ax):
-            ax_copy(it, step).wait_recv()
+        wait_for(part_ax.at[it, pl.ds(0, n_ax - 1)], ax_recv.at[it])
         part_cr[it, me_c] = functools.reduce(jnp.add, [part_ax[it, i] for i in range(n_ax)])
         for step in range(1, n_cr):
             cr_copy(it, step).start()
@@ -197,8 +219,7 @@
         if last:
             gathered = [0.0] * 9
             for d in (1, 2):
-                if it == ITERS - 1:
-                    guarded(d, lambda d=d: rows_copy(d, True).wait_recv())
+                guarded(d, lambda d=d: wait_for(rows_in.at[d], rows_recv.at[d]))
                 rows = rows_in[d]
                 fields = [near_velocity[d], near[d], near_direction[d]]
                 stack = jnp.concatenate([part for f in fields for part in chunks(f)], axis=0)
@@ -217,8 +238,7 @@
                     part = jnp.where(mine, found[n * blocks:(n + 1) * blocks], 0.0)
                     gathered[n] = gathered[n] + jnp.sum(part, axis=0, keepdims=True)
 
-        for d in range(4):
-            guarded(d, lambda d=d: ret_copy(it, d, True).wait_recv())
+        arrived_all(ret_in.at[it], ret_recv.at[it])
         product = drag3 * residual + ret_out[it, CENTRE * blocks:(CENTRE + 1) * blocks]
         for d in range(4):
             product = product + ret_in[it, d]
@@ -227,8 +247,7 @@
             for d in range(4):
                 guarded(d, lambda d=d: halo_copy(it + 1, d).start())
 
-        for step in range(1, n_cr):
-            cr_copy(it, step).wait_recv()
+        wait_for(part_cr.at[it, pl.ds(0, n_cr - 1)], cr_recv.at[it])
         summed = functools.reduce(jnp.add, [part_cr[it, i] for i in range(n_cr)])
         norm, energy, cross = [jnp.sum(s, axis=1, keepdims=True) for s in chunks(summed)]
         if it:
@@ -247,8 +266,8 @@
         if last:
             break
         track = [follow(c, t) for c, t in zip(coupled, track)]
+        arrived_all(halo.at[it + 1], halo_recv.at[it + 1])
         for d in range(4):
-            guarded(d, lambda d=d: halo_copy(it + 1, d, True).wait_recv())
             near_image[d] = follow(halo[it + 1, d], near_image[d])
             if d in (1, 2):
                 near_direction[d] = follow(near[d], near_direction[d])
@@ -259,23 +278,26 @@
     for c in range(3):
         vel_ref[c] = chunks(velocity)[c]
         res_ref[c] = chunks(residual)[c]
-    sub = lax.broadcasted_iota(jnp.int32, (8, 128), 0)
-    arrived = jnp.zeros((8, 128), F32)
     for c in range(3):
         row = gathered[c] + alpha * (gathered[3 + c] + beta * gathered[6 + c])
-        arrived = jnp.where(sub == c, row, arrived)
-    arr_ref[...] = pltpu.roll(arrived, 64, 1)[0:3]
+        arr_ref[c] = pltpu.roll(row, 64, 1)
 
     for d in (1, 2):
-        guarded(d, lambda d=d: rows_copy(d).wait_send())
-    for it in range(ITERS):
-        for d in range(4):
-            guarded(d, lambda d=d: halo_copy(it, d).wait_send())
-            guarded(d, lambda d=d: ret_copy(it, d).wait_send())
-        for step in range(1, n_ax):
-            ax_copy(it, step).wait_send()
-        for step in range(1, n_cr):
-            cr_copy(it, step).wait_send()
+        guarded(d, lambda d=d: wait_for(rows_out.at[d], rows_send.at[d]))
+    for d in range(4):
+        guarded(d, lambda d=d: wait_for(own, halo_send.at[d]))
+        guarded(d, lambda d=d: wait_for(own, ret_send.at[d]))
+    wait_for(part_ax.at[:, pl.ds(0, n_ax - 1)], ax_send)
+    wait_for(part_cr.at[:, pl.ds(0, n_cr - 1)], cr_send)
+
+
+def write_out(vel_in, res_in, arr_in, vel_ref, res_ref, arr_ref, sem):
+    moves = ((vel_in, vel_ref), (res_in, res_ref), (arr_in, arr_ref))
+    copies = [pltpu.make_async_copy(a, b, sem.at[n]) for n, (a, b) in enumerate(moves)]
+    for copy in copies:
+        copy.start()
+    for copy in copies:
+        copy.wait()
 
 
 def on_device(n_ax, n_cr, force, self_drag, tiles, tile_ids, mig_rows, mig_count):
@@ -283,18 +305,23 @@
     count = tiles.shape[3]
     field = (blocks, 3 * width)
     vmem = pl.BlockSpec(memory_space=pltpu.VMEM)
-    smem = pl.BlockSpec(memory_space=pltpu.SMEM)
     dma = pltpu.SemaphoreType.DMA
-    velocity, residual, arrivals = pl.pallas_call(
+    hbm = pl.BlockSpec(memory_space=pltpu.HBM)
+    solved = pl.pallas_call(
         functools.partial(kernel, n_ax, n_cr),
         out_shape=(
             jax.ShapeDtypeStruct((3, blocks, width), F32),
             jax.ShapeDtypeStruct((3, blocks, width), F32),
-            jax.ShapeDtypeStruct((3, 2 * mig_rows.shape[3]), F32),
+            jax.ShapeDtypeStruct((3, 1, 2 * mig_rows.shape[3]), F32),
         ),
-        in_specs=[smem, smem, vmem, vmem, pl.BlockSpec(memory_space=pl.ANY), vmem],
+        in_specs=[hbm] * 6,
         out_specs=(vmem, vmem, vmem),
         scratch_shapes=[
+            pltpu.SMEM((blocks, count), jnp.int32),
+            pltpu.SMEM((2,), jnp.int32),
+            pltpu.VMEM((3, blocks, width), F32),
+            pltpu.VMEM((blocks, width), F32),
+            pltpu.VMEM(mig_rows.shape[2:], jnp.int32),
             pltpu.VMEM((blocks, count, width, width), BF16),
             pltpu.VMEM((8 * blocks, 8, width), F32),
             pltpu.VMEM((blocks * count, 8, width), F32),
@@ -307,12 +334,12 @@
             pltpu.VMEM((8, 128), jnp.int32),
             pltpu.VMEM((3, 1, 128), jnp.int32),
             pltpu.VMEM((3, 1, 128), jnp.int32),
-            dma,
-            dma((ITERS, 4)), dma((ITERS, 4)),
-            dma((ITERS, 4)), dma((ITERS, 4)),
+            dma, dma((5,)),
+            dma((4,)), dma((ITERS,)),
+            dma((4,)), dma((ITERS,)),
             dma((3,)), dma((3,)),
-            dma((ITERS, n_ax)), dma((ITERS, n_ax)),
-            dma((ITERS, n_cr)), dma((ITERS, n_cr)),
+            dma, dma((ITERS,)),
+            dma, dma((ITERS,)),
         ],
         compiler_params=pltpu.CompilerParams(
             collective_id=0, has_side_effects=True, vmem_limit_bytes=60 * 1024 * 1024
@@ -326,8 +353,16 @@
         tiles.reshape(tiles.shape[2:]),
         mig_rows.reshape(mig_rows.shape[2:]),
     )
+    velocity, residual, arrivals = pl.pallas_call(
+        write_out,
+        out_shape=tuple(jax.ShapeDtypeStruct(x.shape, x.dtype) for x in solved),
+        in_specs=[hbm] * 3,
+        out_specs=(hbm,) * 3,
+        scratch_shapes=[dma((3,))],
+        name="write_out",
+    )(*solved)
     velocity, residual = jnp.swapaxes(velocity, 0, 1), jnp.swapaxes(residual, 0, 1)
-    return velocity[None, None], residual[None, None], arrivals[None, None]
+    return velocity[None, None], residual[None, None], arrivals[:, 0][None, None]
 
 
 def solution(mesh):

time: 39.3 us -> 35.5 us (0.903)
  local copies, waits for them, and re-layouts: 3.84 us -> 0 us
    unnamed x3 -> x0, local copies, waits for them, and re-layouts: 3.84 us -> none
    pallas_call x0 -> x1, Pallas kernels: none -> 1.92 us  [on_device(): pl.pallas_call(write_out, out_shape=tuple((jax.ShapeDtypeStruct(x.shape,...]
    pallas_call x1, Pallas kernels: 34.5 us -> 32.7 us  [on_device(): pl.pallas_call(functools.partial(kernel, n_ax, n_cr), out_shape=(jax.Shap...]
where the time goes in v2:
time: 35.5 us; the launch traced here: 35.2 us
  Pallas kernels  34.6 us (97%)
  between operations  0.64 us (2%)
    pallas_call x1, Pallas kernels, on_device(): pl.pallas_call(functools.partial(kernel, n_ax, n_cr), out_shape=(jax.Shap...  32.7 us
    pallas_call x1, Pallas kernels, on_device(): pl.pallas_call(write_out, out_shape=tuple((jax.ShapeDtypeStruct(x.shape,...  1.92 us

profile of v2, /device:TPU:0, one launch (start us, length us, event | category | flops | bytes accessed | tf_op | source)
XLA Modules:
  0.0 35.2 jit_solution(14075237827210540829)
XLA Ops:
  0.6 32.7 %cg_solve.1 = (f32[3,8,128]{2,1,0:T(8,128)}, f32[3,8,128]{2,1,0:T(8,128)}, f32[3,1,128]{2,1,0:T(1,128)}) custom-call(s32[8,8]{1,0:T(8,128)} %bitcast.19, s32[2]{0:T(128)} %bitcast.22, f32[3,8,128]{2,1,0:T(8,128)} %bitcast.18, f32[8,128]{1,0:T(8,128)} %bitcast.20, bf16[8,8,128,128]{3,2,1,0:T(8,128)(2,1)} %bitcast.17, s32[2,64]{1,0:T(2,128)} %bitcast.21), custom_call_target="tpu_custom_call" | custom-call | tf_op jit(solution)/shard_map/cg_solve/pallas_call | solution.py:310
  33.3 1.9 %write_out.1 = (f32[3,8,128]{2,1,0:T(8,128)}, f32[3,8,128]{2,1,0:T(8,128)}, f32[3,1,128]{2,1,0:T(1,128)}) custom-call(f32[3,8,128]{2,1,0:T(8,128)} %get-tuple-element.9.vel_in, f32[3,8,128]{2,1,0:T(8,128)} %get-tuple-element.10.res_in, f32[3,1,128]{2,1,0:T(1,128)} %get-tuple-element.11.arr_in), custom_call_target="tpu_custom_call" | custom-call | tf_op jit(solution)/shard_map/write_out/pallas_call | solution.py:356

commit v3 on v2

--- a/solution.py
+++ b/solution.py
@@ -23,7 +23,7 @@
     n_ax, n_cr,
     ids_hbm, count_hbm, force_hbm, drag_hbm, tiles_ref, rows_hbm,
     vel_ref, res_ref, arr_ref,
-    ids_ref, count_ref, force_ref, drag_ref, rows_ref, tile_buf, ext, spread, own, halo, ret_out, ret_in, part_ax, part_cr, mig, rows_out, rows_in,
+    ids_ref, count_ref, force_ref, drag_ref, rows_ref, tile_buf, tile_turned, ext, spread, own, halo, ret_out, ret_in, part_ax, part_cr, mig, rows_out, rows_in,
     tile_sem, small_sem, halo_send, halo_recv, ret_send, ret_recv, rows_send, rows_recv,
     ax_send, ax_recv, cr_send, cr_recv,
 ):
@@ -166,10 +166,13 @@
     track = [None] * blocks
     norm_before = energy_before = None
 
+    load.wait()
+    for b in range(blocks):
+        for k in range(count):
+            tile_turned[b, k * width:(k + 1) * width] = tile_buf[b, k].T
     arrived_all(halo.at[0], halo_recv.at[0])
     for d in range(4):
         near[d] = halo[0, d]
-    load.wait()
 
     for it in range(ITERS):
         last = it == ITERS - 1
@@ -180,9 +183,7 @@
         coupled = []
         for b in range(blocks):
             picked = jnp.concatenate([ext[ids_ref[b, k]] for k in range(count)], axis=1)
-            coupled.append(lax.dot_general(
-                picked.astype(BF16), tile_row(b), (((1,), (1,)), ((), ())), preferred_element_type=F32,
-            ))
+            coupled.append(jnp.dot(picked.astype(BF16), tile_turned[b], preferred_element_type=F32))
 
         square = functools.reduce(jnp.add, chunks(residual * residual))
         sums = [
@@ -310,9 +311,9 @@
     solved = pl.pallas_call(
         functools.partial(kernel, n_ax, n_cr),
         out_shape=(
-            jax.ShapeDtypeStruct((3, blocks, width), F32),
-            jax.ShapeDtypeStruct((3, blocks, width), F32),
-            jax.ShapeDtypeStruct((3, 1, 2 * mig_rows.shape[3]), F32),
+            pltpu.VMEM((3, blocks, width), F32),
+            pltpu.VMEM((3, blocks, width), F32),
+            pltpu.VMEM((3, 1, 2 * mig_rows.shape[3]), F32),
         ),
         in_specs=[hbm] * 6,
         out_specs=(vmem, vmem, vmem),
@@ -323,6 +324,7 @@
             pltpu.VMEM((blocks, width), F32),
             pltpu.VMEM(mig_rows.shape[2:], jnp.int32),
             pltpu.VMEM((blocks, count, width, width), BF16),
+            pltpu.VMEM((blocks, count * width, width), BF16),
             pltpu.VMEM((8 * blocks, 8, width), F32),
             pltpu.VMEM((blocks * count, 8, width), F32),
             pltpu.VMEM((ITERS,) + field, F32),
@@ -356,7 +358,7 @@
     velocity, residual, arrivals = pl.pallas_call(
         write_out,
         out_shape=tuple(jax.ShapeDtypeStruct(x.shape, x.dtype) for x in solved),
-        in_specs=[hbm] * 3,
+        in_specs=[vmem] * 3,
         out_specs=(hbm,) * 3,
         scratch_shapes=[dma((3,))],
         name="write_out",

time: 35.5 us -> 35.4 us (level)
  Pallas kernels: 34.6 us -> 32.7 us
  local copies, waits for them, and re-layouts: 0 us -> 1.78 us
    unnamed x0 -> x6, local copies, waits for them, and re-layouts: none -> 1.78 us
    pallas_call x1, Pallas kernels: 32.7 us -> 31.3 us  [on_device(): pl.pallas_call(functools.partial(kernel, n_ax, n_cr), out_shape=(pltpu.VM...]
    pallas_call x1, Pallas kernels: 1.92 us -> 1.35 us  [on_device(): pl.pallas_call(write_out, out_shape=tuple((jax.ShapeDtypeStruct(x.shape,...]
where the time goes in v3:
time: 35.4 us; the launch traced here: 35.1 us
  Pallas kernels  32.7 us (92%)
  local copies, waits for them, and re-layouts  1.78 us (5%)
  between operations  0.65 us (2%)
    pallas_call x1, Pallas kernels, on_device(): pl.pallas_call(functools.partial(kernel, n_ax, n_cr), out_shape=(pltpu.VM...  31.3 us
    unnamed x6, local copies, waits for them, and re-layouts  1.78 us
    pallas_call x1, Pallas kernels, on_device(): pl.pallas_call(write_out, out_shape=tuple((jax.ShapeDtypeStruct(x.shape,...  1.35 us

profile of v3, /device:TPU:0, one launch (start us, length us, event | category | flops | bytes accessed | tf_op | source)
XLA Modules:
  0.0 35.1 jit_solution(5665812239262206369)
XLA Ops:
  0.6 31.3 %cg_solve.1 = (f32[3,8,128]{2,1,0:T(8,128)S(1)}, f32[3,8,128]{2,1,0:T(8,128)S(1)}, f32[3,1,128]{2,1,0:T(1,128)S(1)}) custom-call(s32[8,8]{1,0:T(8,128)} %bitcast.19, s32[2]{0:T(128)} %bitcast.22, f32[3,8,128]{2,1,0:T(8,128)} %bitcast.18, f32[8,128]{1,0:T(8,128)} %bitcast.20, bf16[8,8,128,128]{3,2,1,0:T(8,128)(2,1)} %bitcast.17, s32[2,64]{1,0:T(2,128)} %bitcast.21), custom_call_target="tpu_custom_call" | custom-call | tf_op jit(solution)/shard_map/cg_solve/pallas_call | solution.py:311
  31.9 0.0 copy-start
  32.0 0.6 %copy-done = f32[3,8,128]{2,1,0:T(8,128)} copy-done((f32[3,8,128]{2,1,0:T(8,128)}, f32[3,8,128]{2,1,0:T(8,128)S(1)}, u32[]{:S(2)}) %copy-start) | copy-done | bytes 12312
  32.5 0.0 copy-start.1
  32.5 0.6 %copy-done.1 = f32[3,8,128]{2,1,0:T(8,128)} copy-done((f32[3,8,128]{2,1,0:T(8,128)}, f32[3,8,128]{2,1,0:T(8,128)S(1)}, u32[]{:S(2)}) %copy-start.1) | copy-done | bytes 12312
  33.1 0.0 copy-start.2
  33.1 0.6 %copy-done.2 = f32[3,1,128]{2,1,0:T(1,128)} copy-done((f32[3,1,128]{2,1,0:T(1,128)}, f32[3,1,128]{2,1,0:T(1,128)S(1)}, u32[]{:S(2)}) %copy-start.2) | copy-done | bytes 1560
  33.7 1.4 %write_out.1 = (f32[3,8,128]{2,1,0:T(8,128)}, f32[3,8,128]{2,1,0:T(8,128)}, f32[3,1,128]{2,1,0:T(1,128)}) custom-call(f32[3,8,128]{2,1,0:T(8,128)} %copy-done, f32[3,8,128]{2,1,0:T(8,128)} %copy-done.1, f32[3,1,128]{2,1,0:T(1,128)} %copy-done.2), custom_call_target="tpu_custom_call" | custom-call | tf_op jit(solution)/shard_map/write_out/pallas_call | solution.py:358
Async XLA Ops:
  31.9 0.6 %copy-start = (f32[3,8,128]{2,1,0:T(8,128)}, f32[3,8,128]{2,1,0:T(8,128)S(1)}, u32[]{:S(2)}) copy-start(f32[3,8,128]{2,1,0:T(8,128)S(1)} %get-tuple-element.9.vel_in) | copy-start | bytes 36868
  32.5 0.6 %copy-start.1 = (f32[3,8,128]{2,1,0:T(8,128)}, f32[3,8,128]{2,1,0:T(8,128)S(1)}, u32[]{:S(2)}) copy-start(f32[3,8,128]{2,1,0:T(8,128)S(1)} %get-tuple-element.10.res_in) | copy-start | bytes 36868
  33.1 0.6 %copy-start.2 = (f32[3,1,128]{2,1,0:T(1,128)}, f32[3,1,128]{2,1,0:T(1,128)S(1)}, u32[]{:S(2)}) copy-start(f32[3,1,128]{2,1,0:T(1,128)S(1)} %get-tuple-element.11.arr_in) | copy-start | bytes 4612

commit v4 on v3

--- a/solution.py
+++ b/solution.py
@@ -169,7 +169,8 @@
     load.wait()
     for b in range(blocks):
         for k in range(count):
-            tile_turned[b, k * width:(k + 1) * width] = tile_buf[b, k].T
+            side = (b % 2) * width
+            tile_turned[b // 2, k * width:(k + 1) * width, side:side + width] = tile_buf[b, k].T
     arrived_all(halo.at[0], halo_recv.at[0])
     for d in range(4):
         near[d] = halo[0, d]
@@ -181,9 +182,12 @@
         for d in range(4):
             place(PLACES[d], near[d])
         coupled = []
-        for b in range(blocks):
-            picked = jnp.concatenate([ext[ids_ref[b, k]] for k in range(count)], axis=1)
-            coupled.append(jnp.dot(picked.astype(BF16), tile_turned[b], preferred_element_type=F32))
+        for b in range(0, blocks, 2):
+            picked = jnp.concatenate([
+                jnp.concatenate([ext[ids_ref[b + s, k]] for k in range(count)], axis=1) for s in range(2)
+            ], axis=0)
+            pair = jnp.dot(picked.astype(BF16), tile_turned[b // 2], preferred_element_type=F32)
+            coupled += [pair[0:8, 0:width], pair[8:16, width:2 * width]]
 
         square = functools.reduce(jnp.add, chunks(residual * residual))
         sums = [
@@ -199,10 +203,17 @@
         for step in range(1, n_ax):
             ax_copy(it, step).start()
 
-        for b in range(blocks):
-            back = jnp.dot(coupled[b].astype(BF16), tile_row(b), preferred_element_type=F32)
+        for b in range(0, blocks, 2):
+            blank = jnp.zeros((8, width), F32)
+            diagonal = jnp.concatenate([
+                jnp.concatenate([coupled[b], blank], axis=1),
+                jnp.concatenate([blank, coupled[b + 1]], axis=1),
+            ], axis=0)
+            both = jnp.concatenate([tile_row(b), tile_row(b + 1)], axis=0)
+            back = jnp.dot(diagonal.astype(BF16), both, preferred_element_type=F32)
             for k in range(count):
-                spread[b * count + k] = back[:, k * width:(k + 1) * width]
+                spread[b * count + k] = back[0:8, k * width:(k + 1) * width]
+                spread[(b + 1) * count + k] = back[8:16, k * width:(k + 1) * width]
         listed_spread = jnp.concatenate([spread[:, c, :] for c in range(3)], axis=1)
         high = listed_spread.astype(BF16)
         low = (listed_spread - high.astype(F32)).astype(BF16)
@@ -324,7 +335,7 @@
             pltpu.VMEM((blocks, width), F32),
             pltpu.VMEM(mig_rows.shape[2:], jnp.int32),
             pltpu.VMEM((blocks, count, width, width), BF16),
-            pltpu.VMEM((blocks, count * width, width), BF16),
+            pltpu.VMEM((blocks // 2, count * width, 2 * width), BF16),
             pltpu.VMEM((8 * blocks, 8, width), F32),
             pltpu.VMEM((blocks * count, 8, width), F32),
             pltpu.VMEM((ITERS,) + field, F32),
@@ -361,6 +372,7 @@
         in_specs=[vmem] * 3,
         out_specs=(hbm,) * 3,
         scratch_shapes=[dma((3,))],
+        compiler_params=pltpu.CompilerParams(vmem_limit_bytes=1024 * 1024),
         name="write_out",
     )(*solved)
     velocity, residual = jnp.swapaxes(velocity, 0, 1), jnp.swapaxes(residual, 0, 1)

time: 35.4 us -> 32.8 us (0.927)
  local copies, waits for them, and re-layouts: 1.78 us -> 0 us
  Pallas kernels: 32.7 us -> 31.9 us
    unnamed x6 -> x0, local copies, waits for them, and re-layouts: 1.78 us -> none
    pallas_call x1, Pallas kernels: 1.35 us -> 0.63 us  [on_device(): pl.pallas_call(write_out, out_shape=tuple((jax.ShapeDtypeStruct(x.shape,...]
where the time goes in v4:
time: 32.8 us; the launch traced here: 32.6 us
  Pallas kernels  31.9 us (97%)
  between operations  0.64 us (2%)
    pallas_call x1, Pallas kernels, on_device(): pl.pallas_call(functools.partial(kernel, n_ax, n_cr), out_shape=(pltpu.VM...  31.3 us

profile of v4, /device:TPU:0, one launch (start us, length us, event | category | flops | bytes accessed | tf_op | source)
XLA Modules:
  0.0 32.6 jit_solution(9564242526122504855)
XLA Ops:
  0.6 31.3 %cg_solve.1 = (f32[3,8,128]{2,1,0:T(8,128)S(1)}, f32[3,8,128]{2,1,0:T(8,128)S(1)}, f32[3,1,128]{2,1,0:T(1,128)S(1)}) custom-call(s32[8,8]{1,0:T(8,128)} %bitcast.19, s32[2]{0:T(128)} %bitcast.22, f32[3,8,128]{2,1,0:T(8,128)} %bitcast.18, f32[8,128]{1,0:T(8,128)} %bitcast.20, bf16[8,8,128,128]{3,2,1,0:T(8,128)(2,1)} %bitcast.17, s32[2,64]{1,0:T(2,128)} %bitcast.21), custom_call_target="tpu_custom_call" | custom-call | tf_op jit(solution)/shard_map/cg_solve/pallas_call | solution.py:322
  31.9 0.6 %write_out.1 = (f32[3,8,128]{2,1,0:T(8,128)}, f32[3,8,128]{2,1,0:T(8,128)}, f32[3,1,128]{2,1,0:T(1,128)}) custom-call(f32[3,8,128]{2,1,0:T(8,128)S(1)} %get-tuple-element.9.vel_in, f32[3,8,128]{2,1,0:T(8,128)S(1)} %get-tuple-element.10.res_in, f32[3,1,128]{2,1,0:T(1,128)S(1)} %get-tuple-element.11.arr_in), custom_call_target="tpu_custom_call" | custom-call | tf_op jit(solution)/shard_map/write_out/pallas_call | solution.py:369

commit v5 on v4

--- a/solution.py
+++ b/solution.py
@@ -8,7 +8,7 @@
 from jax.sharding import PartitionSpec as P
 
 ITERS = 3
-MESH = pl.DeviceIdType.MESH
+LOGICAL = pl.DeviceIdType.LOGICAL
 PLACES = (1, 3, 5, 7)
 CENTRE = 4
 F32 = jnp.float32
@@ -33,11 +33,15 @@
     me_a = lax.axis_index("axial")
     me_c = lax.axis_index("cross")
 
+    me = me_a * n_cr + me_c
+    ax_peers = [jnp.where(me_a + step < n_ax, me + step * n_cr, me + (step - n_ax) * n_cr) for step in range(n_ax)]
+    cr_peers = [jnp.where(me_c + step < n_cr, me + step, me + (step - n_cr)) for step in range(n_cr)]
+
     def ax_peer(step):
-        return {"axial": lax.rem(me_a + step, n_ax)}
+        return ax_peers[step]
 
     def cr_peer(step):
-        return {"cross": lax.rem(me_c + step, n_cr)}
+        return cr_peers[step]
 
     device = (ax_peer(n_ax - 1), cr_peer(n_cr - 1), cr_peer(1), ax_peer(1))
     exists = (None, me_c > 0, me_c + 1 < n_cr, None)
@@ -51,7 +55,7 @@
     def neighbour(src, dst, send, recv, d):
         return pltpu.make_async_remote_copy(
             src_ref=src, dst_ref=dst.at[3 - d], send_sem=send, recv_sem=recv,
-            device_id=device[d], device_id_type=MESH,
+            device_id=device[d], device_id_type=LOGICAL,
         )
 
     def halo_copy(stage, d):
@@ -82,14 +86,14 @@
         return pltpu.make_async_remote_copy(
             src_ref=part_ax.at[it, me_a], dst_ref=part_ax.at[it, me_a],
             send_sem=ax_send, recv_sem=ax_recv.at[it],
-            device_id=ax_peer(step), device_id_type=MESH,
+            device_id=ax_peer(step), device_id_type=LOGICAL,
         )
 
     def cr_copy(it, step):
         return pltpu.make_async_remote_copy(
             src_ref=part_cr.at[it, me_c], dst_ref=part_cr.at[it, me_c],
             send_sem=cr_send, recv_sem=cr_recv.at[it],
-            device_id=cr_peer(step), device_id_type=MESH,
+            device_id=cr_peer(step), device_id_type=LOGICAL,
         )
 
     fetched = (
@@ -102,9 +106,9 @@
 
     barrier = pltpu.get_barrier_semaphore()
     for step in range(1, n_ax):
-        pl.semaphore_signal(barrier, inc=1, device_id=ax_peer(step), device_id_type=MESH)
+        pl.semaphore_signal(barrier, inc=1, device_id=ax_peer(step), device_id_type=LOGICAL)
     for step in range(1, n_cr):
-        pl.semaphore_signal(barrier, inc=1, device_id=cr_peer(step), device_id_type=MESH)
+        pl.semaphore_signal(barrier, inc=1, device_id=cr_peer(step), device_id_type=LOGICAL)
 
     load = pltpu.make_async_copy(tiles_ref, tile_buf, tile_sem)
     load.start()
@@ -212,9 +216,9 @@
             both = jnp.concatenate([tile_row(b), tile_row(b + 1)], axis=0)
             back = jnp.dot(diagonal.astype(BF16), both, preferred_element_type=F32)
             for k in range(count):
-                spread[b * count + k] = back[0:8, k * width:(k + 1) * width]
-                spread[(b + 1) * count + k] = back[8:16, k * width:(k + 1) * width]
-        listed_spread = jnp.concatenate([spread[:, c, :] for c in range(3)], axis=1)
+                spread[pl.ds((b * count + k) * 8, 8), :] = back[0:8, k * width:(k + 1) * width]
+                spread[pl.ds(((b + 1) * count + k) * 8, 8), :] = back[8:16, k * width:(k + 1) * width]
+        listed_spread = jnp.concatenate([spread[pl.ds(c, pairs, 8), :] for c in range(3)], axis=1)
         high = listed_spread.astype(BF16)
         low = (listed_spread - high.astype(F32)).astype(BF16)
         ret_out[it] = jnp.dot(
@@ -337,7 +341,7 @@
             pltpu.VMEM((blocks, count, width, width), BF16),
             pltpu.VMEM((blocks // 2, count * width, 2 * width), BF16),
             pltpu.VMEM((8 * blocks, 8, width), F32),
-            pltpu.VMEM((blocks * count, 8, width), F32),
+            pltpu.VMEM((blocks * count * 8, width), F32),
             pltpu.VMEM((ITERS,) + field, F32),
             pltpu.VMEM((ITERS, 4) + field, F32),
             pltpu.VMEM((ITERS, 8 * blocks, 3 * width), F32),

time: 32.8 us -> 32.8 us (level)
  no operation moved by 1% of the time
where the time goes in v5:
time: 32.8 us; the launch traced here: 32.5 us
  Pallas kernels  31.9 us (97%)
  between operations  0.64 us (2%)
    pallas_call x1, Pallas kernels, on_device(): pl.pallas_call(functools.partial(kernel, n_ax, n_cr), out_shape=(pltpu.VM...  31.3 us

profile of v5, /device:TPU:0, one launch (start us, length us, event | category | flops | bytes accessed | tf_op | source)
XLA Modules:
  0.0 32.5 jit_solution(8874424815645835301)
XLA Ops:
  0.6 31.3 %cg_solve.1 = (f32[3,8,128]{2,1,0:T(8,128)S(1)}, f32[3,8,128]{2,1,0:T(8,128)S(1)}, f32[3,1,128]{2,1,0:T(1,128)S(1)}) custom-call(s32[8,8]{1,0:T(8,128)} %bitcast.19, s32[2]{0:T(128)} %bitcast.22, f32[3,8,128]{2,1,0:T(8,128)} %bitcast.18, f32[8,128]{1,0:T(8,128)} %bitcast.20, bf16[8,8,128,128]{3,2,1,0:T(8,128)(2,1)} %bitcast.17, s32[2,64]{1,0:T(2,128)} %bitcast.21), custom_call_target="tpu_custom_call" | custom-call | tf_op jit(solution)/shard_map/cg_solve/pallas_call | solution.py:326
  31.9 0.6 %write_out.1 = (f32[3,8,128]{2,1,0:T(8,128)}, f32[3,8,128]{2,1,0:T(8,128)}, f32[3,1,128]{2,1,0:T(1,128)}) custom-call(f32[3,8,128]{2,1,0:T(8,128)S(1)} %get-tuple-element.9.vel_in, f32[3,8,128]{2,1,0:T(8,128)S(1)} %get-tuple-element.10.res_in, f32[3,1,128]{2,1,0:T(1,128)S(1)} %get-tuple-element.11.arr_in), custom_call_target="tpu_custom_call" | custom-call | tf_op jit(solution)/shard_map/write_out/pallas_call | solution.py:373

commit v6 on v5

--- a/solution.py
+++ b/solution.py
@@ -23,9 +23,9 @@
     n_ax, n_cr,
     ids_hbm, count_hbm, force_hbm, drag_hbm, tiles_ref, rows_hbm,
     vel_ref, res_ref, arr_ref,
-    ids_ref, count_ref, force_ref, drag_ref, rows_ref, tile_buf, tile_turned, ext, spread, own, halo, ret_out, ret_in, part_ax, part_cr, mig, rows_out, rows_in,
+    ids_ref, count_ref, force_ref, drag_ref, rows_ref, tile_buf, tile_turned, ext, spread, own, halo, ret_out, ret_in, parts, mig, rows_out, rows_in,
     tile_sem, small_sem, halo_send, halo_recv, ret_send, ret_recv, rows_send, rows_recv,
-    ax_send, ax_recv, cr_send, cr_recv,
+    sum_send, sum_recv,
 ):
     blocks, count, width = tiles_ref.shape[0], tiles_ref.shape[1], tiles_ref.shape[2]
     pairs = blocks * count
@@ -34,16 +34,12 @@
     me_c = lax.axis_index("cross")
 
     me = me_a * n_cr + me_c
-    ax_peers = [jnp.where(me_a + step < n_ax, me + step * n_cr, me + (step - n_ax) * n_cr) for step in range(n_ax)]
-    cr_peers = [jnp.where(me_c + step < n_cr, me + step, me + (step - n_cr)) for step in range(n_cr)]
-
-    def ax_peer(step):
-        return ax_peers[step]
-
-    def cr_peer(step):
-        return cr_peers[step]
-
-    device = (ax_peer(n_ax - 1), cr_peer(n_cr - 1), cr_peer(1), ax_peer(1))
+    device = (
+        jnp.where(me_a > 0, me - n_cr, me + (n_ax - 1) * n_cr),
+        me - 1,
+        me + 1,
+        jnp.where(me_a + 1 < n_ax, me + n_cr, me - (n_ax - 1) * n_cr),
+    )
     exists = (None, me_c > 0, me_c + 1 < n_cr, None)
 
     def guarded(d, act):
@@ -82,19 +78,23 @@
         def _():
             wait_for(ref.at[pl.ds(0, 3)], sem)
 
-    def ax_copy(it, step):
+    everyone = n_ax * n_cr
+
+    def peer(step):
+        return jnp.where(me + step < everyone, me + step, me + step - everyone)
+
+    def sum_copy(it, step):
         return pltpu.make_async_remote_copy(
-            src_ref=part_ax.at[it, me_a], dst_ref=part_ax.at[it, me_a],
-            send_sem=ax_send, recv_sem=ax_recv.at[it],
-            device_id=ax_peer(step), device_id_type=LOGICAL,
+            src_ref=parts.at[it, me], dst_ref=parts.at[it, me],
+            send_sem=sum_send, recv_sem=sum_recv.at[it],
+            device_id=peer(step), device_id_type=LOGICAL,
         )
 
-    def cr_copy(it, step):
-        return pltpu.make_async_remote_copy(
-            src_ref=part_cr.at[it, me_c], dst_ref=part_cr.at[it, me_c],
-            send_sem=cr_send, recv_sem=cr_recv.at[it],
-            device_id=cr_peer(step), device_id_type=LOGICAL,
-        )
+    def each_peer(act):
+        def body(step, carry):
+            act(step)
+            return carry
+        lax.fori_loop(1, everyone, body, 0)
 
     fetched = (
         (force_hbm, force_ref), (ids_hbm, ids_ref), (count_hbm, count_ref),
@@ -105,10 +105,7 @@
         copy.start()
 
     barrier = pltpu.get_barrier_semaphore()
-    for step in range(1, n_ax):
-        pl.semaphore_signal(barrier, inc=1, device_id=ax_peer(step), device_id_type=LOGICAL)
-    for step in range(1, n_cr):
-        pl.semaphore_signal(barrier, inc=1, device_id=cr_peer(step), device_id_type=LOGICAL)
+    each_peer(lambda step: pl.semaphore_signal(barrier, inc=1, device_id=peer(step), device_id_type=LOGICAL))
 
     load = pltpu.make_async_copy(tiles_ref, tile_buf, tile_sem)
     load.start()
@@ -132,7 +129,7 @@
                 ret_in[stage, d] = jnp.zeros((blocks, 3 * width), F32)
             rows_in[d] = jnp.full((1, 128), -1, jnp.int32)
 
-    pl.semaphore_wait(barrier, n_ax - 1 + n_cr - 1)
+    pl.semaphore_wait(barrier, everyone - 1)
 
     for d in range(4):
         guarded(d, lambda d=d: halo_copy(0, d).start())
@@ -203,9 +200,11 @@
             sums.append(total([drag * mixed] + [c * t for c, t in zip(coupled, track)]))
         else:
             sums.append(jnp.zeros((1, 128), F32))
-        part_ax[it, me_a] = jnp.concatenate(sums, axis=1)
-        for step in range(1, n_ax):
-            ax_copy(it, step).start()
+        packed = jnp.zeros((1, 128), F32)
+        for n, row in enumerate(sums):
+            packed = jnp.where(lane == n, jnp.sum(row, axis=1, keepdims=True), packed)
+        parts[it, me] = packed
+        each_peer(lambda step: sum_copy(it, step).start())
 
         for b in range(0, blocks, 2):
             blank = jnp.zeros((8, width), F32)
@@ -226,11 +225,6 @@
         )
         for d in range(4):
             guarded(d, lambda d=d: ret_copy(it, d).start())
-
-        wait_for(part_ax.at[it, pl.ds(0, n_ax - 1)], ax_recv.at[it])
-        part_cr[it, me_c] = functools.reduce(jnp.add, [part_ax[it, i] for i in range(n_ax)])
-        for step in range(1, n_cr):
-            cr_copy(it, step).start()
 
         if last:
             gathered = [0.0] * 9
@@ -263,9 +257,11 @@
             for d in range(4):
                 guarded(d, lambda d=d: halo_copy(it + 1, d).start())
 
-        wait_for(part_cr.at[it, pl.ds(0, n_cr - 1)], cr_recv.at[it])
-        summed = functools.reduce(jnp.add, [part_cr[it, i] for i in range(n_cr)])
-        norm, energy, cross = [jnp.sum(s, axis=1, keepdims=True) for s in chunks(summed)]
+        wait_for(parts.at[it, pl.ds(0, everyone - 1)], sum_recv.at[it])
+        summed = jnp.sum(parts[it], axis=0)
+        norm, energy, cross = [
+            jnp.sum(jnp.where(lane == n, summed, 0.0), axis=1, keepdims=True) for n in range(3)
+        ]
         if it:
             beta = norm / norm_before
             energy = energy + 2.0 * beta * cross + beta * beta * energy_before
@@ -303,8 +299,7 @@
     for d in range(4):
         guarded(d, lambda d=d: wait_for(own, halo_send.at[d]))
         guarded(d, lambda d=d: wait_for(own, ret_send.at[d]))
-    wait_for(part_ax.at[:, pl.ds(0, n_ax - 1)], ax_send)
-    wait_for(part_cr.at[:, pl.ds(0, n_cr - 1)], cr_send)
+    wait_for(parts.at[:, pl.ds(0, everyone - 1)], sum_send)
 
 
 def write_out(vel_in, res_in, arr_in, vel_ref, res_ref, arr_ref, sem):
@@ -346,8 +341,7 @@
             pltpu.VMEM((ITERS, 4) + field, F32),
             pltpu.VMEM((ITERS, 8 * blocks, 3 * width), F32),
             pltpu.VMEM((ITERS, 4) + field, F32),
-            pltpu.VMEM((ITERS, n_ax, 1, 384), F32),
-            pltpu.VMEM((ITERS, n_cr, 1, 384), F32),
+            pltpu.VMEM((ITERS, n_ax * n_cr, 1, 128), F32),
             pltpu.VMEM((8, 128), jnp.int32),
             pltpu.VMEM((3, 1, 128), jnp.int32),
             pltpu.VMEM((3, 1, 128), jnp.int32),
@@ -355,7 +349,6 @@
             dma((4,)), dma((ITERS,)),
             dma((4,)), dma((ITERS,)),
             dma((3,)), dma((3,)),
-            dma, dma((ITERS,)),
             dma, dma((ITERS,)),
         ],
         compiler_params=pltpu.CompilerParams(

time: 32.8 us -> 32.1 us (0.979)
  Pallas kernels: 31.9 us -> 31.3 us
    pallas_call x1, Pallas kernels: 31.3 us -> 30.6 us  [on_device(): pl.pallas_call(functools.partial(kernel, n_ax, n_cr), out_shape=(pltpu.VM...]
where the time goes in v6:
time: 32.1 us; the launch traced here: 31.9 us
  Pallas kernels  31.3 us (98%)
  between operations  0.64 us (2%)
    pallas_call x1, Pallas kernels, on_device(): pl.pallas_call(functools.partial(kernel, n_ax, n_cr), out_shape=(pltpu.VM...  30.6 us

profile of v6, /device:TPU:0, one launch (start us, length us, event | category | flops | bytes accessed | tf_op | source)
XLA Modules:
  0.0 31.9 jit_solution(1863000314482522952)
XLA Ops:
  0.6 30.6 %cg_solve.1 = (f32[3,8,128]{2,1,0:T(8,128)S(1)}, f32[3,8,128]{2,1,0:T(8,128)S(1)}, f32[3,1,128]{2,1,0:T(1,128)S(1)}) custom-call(s32[8,8]{1,0:T(8,128)} %bitcast.19, s32[2]{0:T(128)} %bitcast.22, f32[3,8,128]{2,1,0:T(8,128)} %bitcast.18, f32[8,128]{1,0:T(8,128)} %bitcast.20, bf16[8,8,128,128]{3,2,1,0:T(8,128)(2,1)} %bitcast.17, s32[2,64]{1,0:T(2,128)} %bitcast.21), custom_call_target="tpu_custom_call" | custom-call | tf_op jit(solution)/shard_map/cg_solve/pallas_call | solution.py:321
  31.3 0.6 %write_out.1 = (f32[3,8,128]{2,1,0:T(8,128)}, f32[3,8,128]{2,1,0:T(8,128)}, f32[3,1,128]{2,1,0:T(1,128)}) custom-call(f32[3,8,128]{2,1,0:T(8,128)S(1)} %get-tuple-element.9.vel_in, f32[3,8,128]{2,1,0:T(8,128)S(1)} %get-tuple-element.10.res_in, f32[3,1,128]{2,1,0:T(1,128)S(1)} %get-tuple-element.11.arr_in), custom_call_target="tpu_custom_call" | custom-call | tf_op jit(solution)/shard_map/write_out/pallas_call | solution.py:366

commit v7 on v6

--- a/solution.py
+++ b/solution.py
@@ -204,7 +204,8 @@
         for n, row in enumerate(sums):
             packed = jnp.where(lane == n, jnp.sum(row, axis=1, keepdims=True), packed)
         parts[it, me] = packed
-        each_peer(lambda step: sum_copy(it, step).start())
+        if last:
+            each_peer(lambda step: sum_copy(it, step).start())
 
         for b in range(0, blocks, 2):
             blank = jnp.zeros((8, width), F32)
@@ -225,6 +226,8 @@
         )
         for d in range(4):
             guarded(d, lambda d=d: ret_copy(it, d).start())
+        if not last:
+            each_peer(lambda step: sum_copy(it, step).start())
 
         if last:
             gathered = [0.0] * 9

time: 32.1 us -> 31.2 us (0.972)
  Pallas kernels: 31.3 us -> 30.3 us
    pallas_call x1, Pallas kernels: 30.6 us -> 29.7 us  [on_device(): pl.pallas_call(functools.partial(kernel, n_ax, n_cr), out_shape=(pltpu.VM...]
where the time goes in v7:
time: 31.2 us; the launch traced here: 31 us
  Pallas kernels  30.3 us (97%)
  between operations  0.64 us (2%)
    pallas_call x1, Pallas kernels, on_device(): pl.pallas_call(functools.partial(kernel, n_ax, n_cr), out_shape=(pltpu.VM...  29.7 us
    pallas_call x1, Pallas kernels, on_device(): pl.pallas_call(write_out, out_shape=tuple((jax.ShapeDtypeStruct(x.shape,...  0.63 us

profile of v7, /device:TPU:0, one launch (start us, length us, event | category | flops | bytes accessed | tf_op | source)
XLA Modules:
  0.0 31.0 jit_solution(12512236750290748130)
XLA Ops:
  0.6 29.7 %cg_solve.1 = (f32[3,8,128]{2,1,0:T(8,128)S(1)}, f32[3,8,128]{2,1,0:T(8,128)S(1)}, f32[3,1,128]{2,1,0:T(1,128)S(1)}) custom-call(s32[8,8]{1,0:T(8,128)} %bitcast.19, s32[2]{0:T(128)} %bitcast.22, f32[3,8,128]{2,1,0:T(8,128)} %bitcast.18, f32[8,128]{1,0:T(8,128)} %bitcast.20, bf16[8,8,128,128]{3,2,1,0:T(8,128)(2,1)} %bitcast.17, s32[2,64]{1,0:T(2,128)} %bitcast.21), custom_call_target="tpu_custom_call" | custom-call | tf_op jit(solution)/shard_map/cg_solve/pallas_call | solution.py:324
  30.3 0.6 %write_out.1 = (f32[3,8,128]{2,1,0:T(8,128)}, f32[3,8,128]{2,1,0:T(8,128)}, f32[3,1,128]{2,1,0:T(1,128)}) custom-call(f32[3,8,128]{2,1,0:T(8,128)S(1)} %get-tuple-element.9.vel_in, f32[3,8,128]{2,1,0:T(8,128)S(1)} %get-tuple-element.10.res_in, f32[3,1,128]{2,1,0:T(1,128)S(1)} %get-tuple-element.11.arr_in), custom_call_target="tpu_custom_call" | custom-call | tf_op jit(solution)/shard_map/write_out/pallas_call | solution.py:369

commit v8 on v7

--- a/solution.py
+++ b/solution.py
@@ -94,19 +94,24 @@
         def body(step, carry):
             act(step)
             return carry
-        lax.fori_loop(1, everyone, body, 0)
+        if everyone > 64:
+            lax.fori_loop(1, everyone, body, 0)
+        else:
+            for step in range(1, everyone):
+                act(step)
 
     fetched = (
         (force_hbm, force_ref), (ids_hbm, ids_ref), (count_hbm, count_ref),
         (drag_hbm, drag_ref), (rows_hbm, rows_ref),
     )
     small = [pltpu.make_async_copy(a, b, small_sem.at[n]) for n, (a, b) in enumerate(fetched)]
-    for copy in small:
-        copy.start()
+    small[0].start()
 
     barrier = pltpu.get_barrier_semaphore()
     each_peer(lambda step: pl.semaphore_signal(barrier, inc=1, device_id=peer(step), device_id_type=LOGICAL))
 
+    for copy in small[1:]:
+        copy.start()
     load = pltpu.make_async_copy(tiles_ref, tile_buf, tile_sem)
     load.start()
     for copy in small:

time: 31.2 us -> 31.2 us (level)
  no operation moved by 1% of the time
where the time goes in v8:
time: 31.2 us; the launch traced here: 30.9 us
  Pallas kernels  30.3 us (97%)
  between operations  0.64 us (2%)
    pallas_call x1, Pallas kernels, on_device(): pl.pallas_call(functools.partial(kernel, n_ax, n_cr), out_shape=(pltpu.VM...  29.6 us
    pallas_call x1, Pallas kernels, on_device(): pl.pallas_call(write_out, out_shape=tuple((jax.ShapeDtypeStruct(x.shape,...  0.63 us

profile of v8, /device:TPU:0, one launch (start us, length us, event | category | flops | bytes accessed | tf_op | source)
XLA Modules:
  0.0 30.9 jit_solution(6422227739698844960)
XLA Ops:
  0.6 29.6 %cg_solve.1 = (f32[3,8,128]{2,1,0:T(8,128)S(1)}, f32[3,8,128]{2,1,0:T(8,128)S(1)}, f32[3,1,128]{2,1,0:T(1,128)S(1)}) custom-call(s32[8,8]{1,0:T(8,128)} %bitcast.19, s32[2]{0:T(128)} %bitcast.22, f32[3,8,128]{2,1,0:T(8,128)} %bitcast.18, f32[8,128]{1,0:T(8,128)} %bitcast.20, bf16[8,8,128,128]{3,2,1,0:T(8,128)(2,1)} %bitcast.17, s32[2,64]{1,0:T(2,128)} %bitcast.21), custom_call_target="tpu_custom_call" | custom-call | tf_op jit(solution)/shard_map/cg_solve/pallas_call | solution.py:329
  30.3 0.6 %write_out.1 = (f32[3,8,128]{2,1,0:T(8,128)}, f32[3,8,128]{2,1,0:T(8,128)}, f32[3,1,128]{2,1,0:T(1,128)}) custom-call(f32[3,8,128]{2,1,0:T(8,128)S(1)} %get-tuple-element.9.vel_in, f32[3,8,128]{2,1,0:T(8,128)S(1)} %get-tuple-element.10.res_in, f32[3,1,128]{2,1,0:T(1,128)S(1)} %get-tuple-element.11.arr_in), custom_call_target="tpu_custom_call" | custom-call | tf_op jit(solution)/shard_map/write_out/pallas_call | solution.py:374

commit v9 on v8

--- a/solution.py
+++ b/solution.py
@@ -209,9 +209,6 @@
         for n, row in enumerate(sums):
             packed = jnp.where(lane == n, jnp.sum(row, axis=1, keepdims=True), packed)
         parts[it, me] = packed
-        if last:
-            each_peer(lambda step: sum_copy(it, step).start())
-
         for b in range(0, blocks, 2):
             blank = jnp.zeros((8, width), F32)
             diagonal = jnp.concatenate([
@@ -231,8 +228,7 @@
         )
         for d in range(4):
             guarded(d, lambda d=d: ret_copy(it, d).start())
-        if not last:
-            each_peer(lambda step: sum_copy(it, step).start())
+        each_peer(lambda step: sum_copy(it, step).start())
 
         if last:
             gathered = [0.0] * 9

time: 31.2 us -> 30.9 us (level)
  no operation moved by 1% of the time
where the time goes in v9:
time: 30.9 us; the launch traced here: 30.7 us
  Pallas kernels  30.1 us (97%)
  between operations  0.64 us (2%)
    pallas_call x1, Pallas kernels, on_device(): pl.pallas_call(functools.partial(kernel, n_ax, n_cr), out_shape=(pltpu.VM...  29.4 us
    pallas_call x1, Pallas kernels, on_device(): pl.pallas_call(write_out, out_shape=tuple((jax.ShapeDtypeStruct(x.shape,...  0.63 us

profile of v9, /device:TPU:0, one launch (start us, length us, event | category | flops | bytes accessed | tf_op | source)
XLA Modules:
  0.0 30.7 jit_solution(7094231848163651770)
XLA Ops:
  0.6 29.4 %cg_solve.1 = (f32[3,8,128]{2,1,0:T(8,128)S(1)}, f32[3,8,128]{2,1,0:T(8,128)S(1)}, f32[3,1,128]{2,1,0:T(1,128)S(1)}) custom-call(s32[8,8]{1,0:T(8,128)} %bitcast.19, s32[2]{0:T(128)} %bitcast.22, f32[3,8,128]{2,1,0:T(8,128)} %bitcast.18, f32[8,128]{1,0:T(8,128)} %bitcast.20, bf16[8,8,128,128]{3,2,1,0:T(8,128)(2,1)} %bitcast.17, s32[2,64]{1,0:T(2,128)} %bitcast.21), custom_call_target="tpu_custom_call" | custom-call | tf_op jit(solution)/shard_map/cg_solve/pallas_call | solution.py:325
  30.1 0.6 %write_out.1 = (f32[3,8,128]{2,1,0:T(8,128)}, f32[3,8,128]{2,1,0:T(8,128)}, f32[3,1,128]{2,1,0:T(1,128)}) custom-call(f32[3,8,128]{2,1,0:T(8,128)S(1)} %get-tuple-element.9.vel_in, f32[3,8,128]{2,1,0:T(8,128)S(1)} %get-tuple-element.10.res_in, f32[3,1,128]{2,1,0:T(1,128)S(1)} %get-tuple-element.11.arr_in), custom_call_target="tpu_custom_call" | custom-call | tf_op jit(solution)/shard_map/write_out/pallas_call | solution.py:370
